TPU v7x, 128 devices: a whole 4x4x4 slice. The times are simulated.
128 devices in a mesh: tok: 4 (over z), lat: 32 (over y, x, core).
Axes of the slice: x: 4, y: 4, z: 4, core: 2. Of those that a mesh axis runs over, the one named last changes fastest.
Arguments:
- tokens: bfloat16 [1024, 4096], P('tok'), may hold values from -6 to 6
- indices: int32 [1024, 64], replicated, may hold values from 0 to 65535, as said below
- enc_weight: bfloat16 [4096, 65536], P('tok', 'lat'), may hold values from -0.375 to 0.375
- dec_weight: bfloat16 [65536, 4096], P('lat', 'tok'), may hold values from -0.09375 to 0.09375
- enc_bias: float32 [65536], P('lat'), may hold values from -6 to 6
- dec_bias: float32 [4096], P('tok'), may hold values from -3 to 3
Outputs:
- enc_grad: bfloat16 [4096, 65536], P('tok', 'lat')
- dec_grad: bfloat16 [65536, 4096], P('lat', 'tok')
- enc_bias_grad: float32 [65536], P('lat')
- dec_bias_grad: float32 [4096], P('tok')
Inputs may be any that keep to these rules, and one draw needn't show every extreme that they name: `indices`: in every row the 64 entries are distinct, and entry s leaves the remainder s when divided by 64.
All inputs are finite; a program needn't handle non-finite values.
Results may differ from a plain program's by a relative error of at most 0.0058.
Values may be sent and summed in bfloat16 or wider, within the bound.
A program may use at most 64 MiB of HBM per device.

v0:
```python
import jax
import jax.numpy as jnp
from jax import lax
from jax.sharding import PartitionSpec as P


def local(tokens, indices, enc_weight, dec_weight, enc_bias, dec_bias):
    lat_width = enc_weight.shape[1]
    tok_total, slot_count = indices.shape
    band_count = lat_width // slot_count
    local_band = indices // slot_count - lax.axis_index("lat") * band_count
    band_ids = lax.broadcasted_iota(jnp.int32, (1, band_count, 1), 1)
    hot_mask = local_band[:, None, :] == band_ids

    def spread(values):
        return jnp.where(hot_mask, values[:, None, :], jnp.zeros((), values.dtype)).reshape(
            tok_total, lat_width
        )

    def pick_active(dense):
        shaped = dense.reshape(dense.shape[0], band_count, slot_count)
        return jnp.sum(jnp.where(hot_mask, shaped, 0.0), axis=1)

    columns = lax.all_to_all(tokens, "tok", split_axis=1, concat_axis=0, tiled=True)
    partial_pre = jnp.dot(columns, enc_weight, preferred_element_type=jnp.float32)
    picked = pick_active(partial_pre)
    bias_terms = pick_active(jnp.broadcast_to(enc_bias[None, :], (tok_total, lat_width)))
    pre_acts = lax.psum(picked, "tok") + bias_terms
    code_vals = pre_acts.astype(jnp.bfloat16)
    dense_codes = spread(code_vals)
    partial_recon = jnp.dot(dense_codes, dec_weight, preferred_element_type=jnp.float32)
    recon_sum = lax.psum(partial_recon, "lat")
    error_full = recon_sum + dec_bias[None, :] - columns.astype(jnp.float32)
    bias_grad = jnp.sum(error_full, axis=0)
    error_half = error_full.astype(jnp.bfloat16)
    dec_grad = lax.dot_general(
        dense_codes, error_half, (((0,), (0,)), ((), ())), preferred_element_type=jnp.float32
    )
    dense_scores = lax.dot_general(
        error_half, dec_weight, (((1,), (1,)), ((), ())), preferred_element_type=jnp.float32
    )
    picked_grad = pick_active(dense_scores)
    code_grad = lax.psum(picked_grad, "tok")
    dense_grad = spread(code_grad)
    enc_bias_grad = jnp.sum(dense_grad, axis=0)
    enc_grad = lax.dot_general(
        columns,
        dense_grad.astype(jnp.bfloat16),
        (((0,), (0,)), ((), ())),
        preferred_element_type=jnp.float32,
    )
    return (enc_grad.astype(jnp.bfloat16), dec_grad.astype(jnp.bfloat16), enc_bias_grad, bias_grad)


def solution(mesh):
    placed = (P("tok", None), P(), P("tok", "lat"), P("lat", "tok"), P("lat"), P("tok"))
    return jax.shard_map(
        local,
        mesh=mesh,
        in_specs=placed,
        out_specs=(P("tok", "lat"), P("lat", "tok"), P("lat"), P("tok")),
        check_vma=False,
    )
```

profile of v0, /device:TPU:0, one launch (start us, length us, event | category | flops | bytes accessed | tf_op | source)
XLA Modules:
  0.0 289.7 jit_solution(16053656291427719163)
XLA Ops:
  7.2 3.1 %copy.21 = bf16[32,4,8,1024]{3,2,0,1:T(8,128)(2,1)} copy(bf16[32,4,8,1024]{3,2,1,0:T(8,128)(2,1)} %bitcast.40) | data formatting | bytes 4194304 | tf_op jit(solution)/shard_map/all_to_all | solution.py:24
  10.3 5.4 %all-to-all-start = ((bf16[256,4,1024]{2,0,1:T(8,128)(2,1)}), bf16[256,4,1024]{2,0,1:T(8,128)(2,1)S(1)}, u32[]{:S(2)}, u32[]{:S(2)}) async-start(bf16[256,4,1024]{2,0,1:T(8,128)(2,1)} %bitcast.37), calls=%async_computation | async-start | bytes 4194304 | tf_op jit(solution)/shard_map/all_to_all | solution.py:24
  15.9 6.4 %copy.15 = bf16[1024,2048]{0,1:T(8,128)(2,1)} copy(bf16[1024,2048]{1,0:T(8,128)(2,1)} %param.8) | data formatting | bytes 8388608 | tf_op args[2]
  22.3 0.2 fusion.4
  22.5 19.6 %all-to-all-done = bf16[256,4,1024]{2,0,1:T(8,128)(2,1)S(1)} async-done(((bf16[256,4,1024]{2,0,1:T(8,128)(2,1)}), bf16[256,4,1024]{2,0,1:T(8,128)(2,1)S(1)}, u32[]{:S(2)}, u32[]{:S(2)}) %all-to-all-start) | async-done | bytes 2097184 | tf_op jit(solution)/shard_map/all_to_all | solution.py:24
  42.0 7.8 %select_reduce_fusion.3 = f32[1024,64]{0,1:T(8,128)} fusion(s32[1024,64]{0,1:T(8,128)S(1)} %fusion.4, bf16[1024,1024,1]{1,0,2:T(8,128)(2,1)S(1)} %bitcast.34, bf16[32,64,1024]{2,1,0:T(8,128)(2,1)} %bitcast.39), kind=kOutput, calls=%fused_computation.5 | convolution fusion | flops 4301193216 | bytes 6815744 | tf_op jit(solution)/shard_map/dot_general | solution.py:25
  49.9 0.9 select_reduce_fusion.2
  50.8 40.7 %all-reduce.4.cloned.1.call-done = f32[1024,64]{0,1:T(8,128)} async-done(((f32[1024,64]{0,1:T(8,128)}), f32[1024,64]{0,1:T(8,128)}) %all-reduce.4.cloned.1.call-update) | async-done | bytes 262160 | tf_op jit(solution)/shard_map/psum | solution.py:28
  91.4 1.1 add_convert_fusion
  92.6 1.3 fusion
  93.9 2.0 copy-done
  95.9 6.1 %fusion.6 = f32[1024,1024]{1,0:T(8,128)} fusion(bf16[1024,2048]{0,1:T(8,128)(2,1)S(1)} %fusion, bf16[2048,1024]{1,0:T(8,128)(2,1)S(1)} %copy-done.5), kind=kOutput, calls=%fused_computation.23 | convolution fusion | flops 4294967296 | bytes 12582912 | tf_op jit(solution)/shard_map/dot_general | solution.py:31
  102.0 0.2 all-reduce.8.cloned.1.call-start
  102.2 111.7 %all-reduce.6.cloned.1.call-done = f32[1024,1024]{1,0:T(8,128)} async-done(((f32[1024,1024]{1,0:T(8,128)}), f32[1024,1024]{1,0:T(8,128)}) %all-reduce.6.cloned.1.call-update) | async-done | bytes 4194320 | tf_op jit(solution)/shard_map/psum | solution.py:32
  213.9 3.8 %fusion.1 = (f32[1024]{0:T(1024)}, bf16[1024,1024]{1,0:T(8,128)(2,1)S(1)}) fusion(f32[1024,1024]{1,0:T(8,128)} %all-reduce.6.cloned.1.call-done, f32[1024]{0:T(1024)S(1)} %copy-done.4, bf16[256,4,1024]{2,0,1:T(8,128)(2,1)S(1)} %all-to-all-done), kind=kLoop, calls=%fused_computation.11 | loop fusion | flops 5241856 | bytes 8396800 | tf_op jit(solution)/shard_map/reduce_sum | solution.py:34
  217.7 4.6 %fusion.7 = f32[1024,2048]{0,1:T(8,128)S(1)} fusion(bf16[1024,1024]{1,0:T(8,128)(2,1)S(1)} %get-tuple-element.13, bf16[2048,1024]{1,0:T(8,128)(2,1)S(1)} %copy-done.6), kind=kOutput, calls=%fused_computation.24 | convolution fusion | flops 4294967296 | bytes 14680064 | tf_op jit(solution)/shard_map/dot_general | solution.py:39
  222.4 1.8 select_reduce_fusion.1
  224.2 9.4 %convolution_convert_fusion = bf16[2048,1024]{1,0:T(8,128)(2,1)} fusion(bf16[1024,2048]{0,1:T(8,128)(2,1)} %copy-done, bf16[1024,1024]{1,0:T(8,128)(2,1)} %copy-done.1), kind=kOutput, calls=%fused_computation.10 | convolution fusion | flops 4297064448 | bytes 10485760 | tf_op jit(solution)/shard_map/dot_general | solution.py:36
  233.6 32.3 %all-reduce.8.cloned.1.call-done = f32[1024,64]{0,1:T(8,128)} async-done(((f32[1024,64]{0,1:T(8,128)}), f32[1024,64]{0,1:T(8,128)}) %all-reduce.8.cloned.1.call-update) | async-done | bytes 262160 | tf_op jit(solution)/shard_map/psum | solution.py:43
  265.9 1.9 select_reduce_fusion
  267.8 0.7 reduce_sum.51
  268.5 2.2 select_convert_fusion
  270.7 6.0 %convert_bitcast_fusion = bf16[1024,2048]{0,1:T(8,128)(2,1)} fusion(bf16[1024,2048]{0,1:T(8,128)(2,1)S(1)} %bitcast.38, bf16[1024,1024]{1,0:T(8,128)(2,1)S(1)} %bitcast.35), kind=kOutput, calls=%fused_computation.8 | convolution fusion | flops 4297064448 | bytes 10485760 | tf_op jit(solution)/shard_map/dot_general | solution.py:46
  276.7 6.4 %copy.17 = bf16[1024,2048]{1,0:T(8,128)(2,1)} copy(bf16[1024,2048]{0,1:T(8,128)(2,1)} %convert_bitcast_fusion) | data formatting | bytes 8388608
  (21 shorter events, 0.3 us)
Async XLA Ops:
  7.2 8.5 %copy-start.3 = (f32[2048]{0:T(1024)S(1)}, f32[2048]{0:T(1024)}, u32[]{:S(2)}) copy-start(f32[2048]{0:T(1024)} %param.10) | copy-start | bytes 24580
  10.3 31.7 %all-to-all-start = ((bf16[256,4,1024]{2,0,1:T(8,128)(2,1)}), bf16[256,4,1024]{2,0,1:T(8,128)(2,1)S(1)}, u32[]{:S(2)}, u32[]{:S(2)}) async-start(bf16[256,4,1024]{2,0,1:T(8,128)(2,1)} %bitcast.37), calls=%async_computation | async-start | bytes 4194304 | tf_op jit(solution)/shard_map/all_to_all | solution.py:24
  15.7 75.7 %all-reduce.4.cloned.1.call-start = ((), (), s32[]{:S(2)}) async-start(), calls=%async_computation.1 | async-start | bytes 524288 | tf_op jit(solution)/shard_map/psum | solution.py:28
  15.9 6.4 %copy-start.2 = (s32[1024,64]{0,1:T(8,128)S(1)}, s32[1024,64]{0,1:T(8,128)}, u32[]{:S(2)}) copy-start(s32[1024,64]{0,1:T(8,128)} %param.7) | copy-start | bytes 786436
  49.9 164.1 %all-reduce.6.cloned.1.call-start = ((), (), s32[]{:S(2)}) async-start(), calls=%async_computation.2 | async-start | bytes 8388608 | tf_op jit(solution)/shard_map/psum | solution.py:32
  91.4 4.4 %copy-start.5 = (bf16[2048,1024]{1,0:T(8,128)(2,1)S(1)}, bf16[2048,1024]{1,0:T(8,128)(2,1)}, u32[]{:S(2)}) copy-start(bf16[2048,1024]{1,0:T(8,128)(2,1)} %param.9) | copy-start | bytes 12582916
  93.9 2.0 copy-start
  101.9 112.0 %copy-start.4 = (f32[1024]{0:T(1024)S(1)}, f32[1024]{0:T(1024)}, u32[]{:S(2)}) copy-start(f32[1024]{0:T(1024)} %param.11) | copy-start | bytes 12292
  102.0 163.9 %all-reduce.8.cloned.1.call-start = ((), (), s32[]{:S(2)}) async-start(), calls=%async_computation.3 | async-start | bytes 524288 | tf_op jit(solution)/shard_map/psum | solution.py:43
  213.9 3.8 %copy-start.6 = (bf16[2048,1024]{1,0:T(8,128)(2,1)S(1)}, bf16[2048,1024]{1,0:T(8,128)(2,1)}, u32[]{:S(2)}) copy-start(bf16[2048,1024]{1,0:T(8,128)(2,1)} %param.9) | copy-start | bytes 12582916
  217.7 4.6 %copy-start.1 = (bf16[1024,1024]{1,0:T(8,128)(2,1)}, bf16[1024,1024]{1,0:T(8,128)(2,1)S(1)}, u32[]{:S(2)}) copy-start(bf16[1024,1024]{1,0:T(8,128)(2,1)S(1)} %get-tuple-element.13) | copy-start | bytes 6291460
Sparse Core Ops, SparseCore 0:
  50.0 41.4 all-reduce.3
  102.1 111.8 all-reduce.5
  224.3 41.5 all-reduce.7
where the time goes:
time: 290 us
  waiting for transfers between devices  204 us (70%)
  matrix products  33.9 us (12%)
  local copies, waits for them, and re-layouts  18.8 us (6%)
  between operations  13.8 us (5%)
  other arithmetic  13.1 us (5%)
  starting transfers between devices  5.66 us (2%)
    psum x1, waiting for transfers between devices, local(): recon_sum = lax.psum(partial_recon, 'lat')  112 us
    psum x1, waiting for transfers between devices, local(): pre_acts = lax.psum(picked, 'tok') + bias_terms  40.7 us
    psum x1, waiting for transfers between devices, local(): code_grad = lax.psum(picked_grad, 'tok')  32.3 us
    all_to_all x1, waiting for transfers between devices, local(): lax.all_to_all(tokens, 'tok', split_axis=1, concat_axis=0, tiled=True)  19.6 us
    unnamed x16, local copies, waits for them, and re-layouts  14.9 us
    dot_general x1, matrix products, local(): lax.dot_general(dense_codes, error_half, (((0,), (0,)), ((), ())), prefer...  9.41 us
    dot_general x1, matrix products, local(): jnp.dot(columns, enc_weight, preferred_element_type=jnp.float32)  7.79 us
    dot_general x1, matrix products, local(): jnp.dot(dense_codes, dec_weight, preferred_element_type=jnp.float32)  6.07 us
  transfers between devices with their start and end apart: 4, of which 4 were waited for; matrix products, arithmetic and copies ran while one was open for 6% of the time, Pallas kernels for 0%

commit v1 on v0

v1 whole, which is shorter than its diff:
```python
import functools

import jax
import jax.numpy as jnp
from jax import lax
from jax.experimental import pallas as pl
from jax.experimental.pallas import tpu as pltpu
from jax.sharding import PartitionSpec as P

MESH = pl.DeviceIdType.MESH
F32, BF16, I32 = jnp.float32, jnp.bfloat16, jnp.int32
NT = (((1,), (1,)), ((), ()))
PLANE = tuple((dy, dx) for dy in range(4) for dx in range(4))
ORDER = (1, 3, 2)


def exchange(
    tokens, idx_t, enc, dec, enc_bias, dec_bias,
    cols_out, dec_grad_out, grad_out, bias_out,
    cols, enc_v, dec_v, key, key_t, picked, own_pre, pre_send, pre_recv,
    codes, code2, codes_t, dense, sib_send, sib_recv, part, rs_send, rs_recv,
    err, grad_part, grad_recv, dec_grad_v,
    sem_local, sem_a, sem_f, sem_b, sem_c, sem_s, sem_r, sem_g, sem_h, sem_d, sem_e, sem_o,
):
    z, lat = lax.axis_index("tok"), lax.axis_index("lat")
    y, x, core = lat // 8, (lat // 2) % 4, lat % 2
    other = 1 - core
    sibling = (z, lat + 1 - 2 * core)

    def along(offset):
        return lax.rem(z + offset, 4)

    def in_plane(dy, dx):
        return (z, lax.rem(y + dy, 4) * 8 + lax.rem(x + dx, 4) * 2 + core)

    def remote(src, dst, sems, index, device):
        return pltpu.make_async_remote_copy(
            src_ref=src, dst_ref=dst, send_sem=sems.at[0, index], recv_sem=sems.at[1, index],
            device_id=device, device_id_type=MESH,
        )

    barrier = pltpu.get_barrier_semaphore()
    peers = [(along(o), lat) for o in ORDER] + [sibling]
    peers += [in_plane(dy, dx) for dy, dx in PLANE if dy or dx]
    for peer in peers:
        pl.semaphore_signal(barrier, inc=1, device_id=peer, device_id_type=MESH)

    own_cols = pltpu.make_async_copy(
        tokens.at[:, pl.ds(pl.multiple_of(1024 * z, 1024), 1024)],
        cols.at[pl.ds(pl.multiple_of(256 * z, 256), 256)], sem_local.at[0])
    load_enc = pltpu.make_async_copy(enc, enc_v, sem_local.at[1])
    load_dec = pltpu.make_async_copy(dec, dec_v, sem_local.at[2])
    own_cols.start()
    load_enc.start()
    load_dec.start()

    pl.semaphore_wait(barrier, len(peers))

    half_rows = pl.ds(pl.multiple_of(128 * core, 128), 128)

    def block_half(block, which):
        return cols.at[pl.ds(pl.multiple_of(256 * block + 128 * which, 128), 128)]

    sends = {}
    for o in ORDER:
        to = along(o)
        sends[o] = remote(
            tokens.at[half_rows, pl.ds(pl.multiple_of(1024 * to, 1024), 1024)],
            block_half(z, core), sem_a, o, (to, lat))
        sends[o].start()

    band_t = lax.shift_right_logical(idx_t[...], 6) - 32 * lat
    key_t[...] = band_t
    odd = (lax.broadcasted_iota(I32, (128, 128), 1) >= 64).astype(I32)
    low = lax.broadcasted_iota(I32, (128, 128), 1) < 64
    for g in range(8):
        piece = band_t[:, 128 * g:128 * g + 128]
        key[128 * g:128 * g + 128, :] = jnp.concatenate([piece, piece], axis=0).T - odd

    own_cols.wait()
    load_enc.wait()

    def pre_block(block, with_bias):
        rows = pl.ds(pl.multiple_of(256 * block, 256), 256)
        picked[...] = jnp.zeros_like(picked)

        @pl.loop(0, 4)
        def _(n):
            base = pl.multiple_of(512 * n, 512)
            scores = jnp.dot(cols[rows, :], enc_v[:, pl.ds(base, 512)], preferred_element_type=F32)
            if with_bias:
                scores = scores + enc_bias[:, pl.ds(base, 512)]
            where = key[rows, :]
            total = picked[...]
            for j in range(4):
                total += jnp.where(where == 8 * n + 2 * j, scores[:, 128 * j:128 * j + 128], 0.0)
            picked[...] = total

        folded = picked[...]
        folded = folded + pltpu.roll(folded, 64, 1)
        return jnp.where(low, folded[:128], folded[128:])

    own_pre[...] = pre_block(z, True)
    forwards = {}
    returns = {}

    def forward(o):
        block = along(4 - o)
        sends[o].wait_recv()
        forwards[o] = remote(block_half(block, core), block_half(block, core), sem_f, o, sibling)
        forwards[o].start()

    def partial(o):
        block = along(4 - o)
        forwards[o].wait_recv()
        pre_send[o] = pre_block(block, False)
        returns[o] = remote(pre_send.at[o], pre_recv.at[o], sem_b, o, (block, lat))
        returns[o].start()

    forward(1)
    forward(3)
    partial(1)
    partial(3)
    forward(2)
    partial(2)

    store_cols = pltpu.make_async_copy(cols, cols_out, sem_local.at[3])
    store_cols.start()

    total = own_pre[...]
    for o in ORDER:
        returns[o].wait_recv()
        total = total + pre_recv[o]
    codes[z] = total.astype(BF16)
    spread_codes = {}
    for o in ORDER:
        spread_codes[o] = remote(codes.at[z], codes.at[z], sem_c, o, (along(o), lat))
        spread_codes[o].start()
    for o in ORDER:
        spread_codes[o].wait_recv()

    for block in range(4):
        packed = codes[block].astype(F32)
        turned = pltpu.roll(packed, 64, 1)
        for high in range(2):
            both = jnp.where(low, turned, packed) if high else jnp.where(low, packed, turned)
            g = 2 * block + high
            code2[128 * g:128 * g + 128, :] = both
            codes_t[:, 128 * g:128 * g + 128] = both.T[:64]

    load_dec.wait()

    def recon(half, chunk, out):
        for pos in range(2):
            dy = (1 + 2 * chunk + pos) % 4
            rows = pl.ds(pl.multiple_of(512 * half + 128 * lax.rem(y + dy, 4), 128), 128)
            where, values = key[rows, :], code2[rows, :]
            for j in range(16):
                dense[128 * pos:128 * pos + 128, 128 * j:128 * j + 128] = jnp.where(
                    where == 2 * j, values, 0.0).astype(BF16)

        @pl.loop(0, 2)
        def _(n):
            base = pl.ds(pl.multiple_of(512 * n, 512), 512)
            out[chunk, :, base] = jnp.dot(dense[...], dec_v[:, base], preferred_element_type=F32)

    to_sibling = {}

    def give(chunk):
        recon(other, chunk, sib_send)
        to_sibling[chunk] = remote(sib_send.at[chunk], sib_recv.at[chunk], sem_s, chunk, sibling)
        to_sibling[chunk].start()

    scatter = {}

    def finish(chunk):
        to_sibling[chunk].wait_recv()

        @pl.loop(0, 8)
        def _(i):
            rows = pl.ds(pl.multiple_of(32 * i, 32), 32)
            total = part[chunk, rows, :] + sib_recv[chunk, rows, :]
            part[chunk, rows, :] = total
            rs_send[chunk, rows, :] = total.astype(BF16)

        for pos in range(2):
            dy = (1 + 2 * chunk + pos) % 4
            for dx in range(4):
                if dy == 0 and dx == 0:
                    continue
                slot = 4 * dy + dx
                rows = pl.ds(pl.multiple_of(128 * pos + 32 * lax.rem(x + dx, 4), 32), 32)
                scatter[slot] = remote(rs_send.at[chunk, rows], rs_recv.at[slot], sem_r, slot, in_plane(dy, dx))
                scatter[slot].start()

    give(0)
    recon(core, 0, part)
    give(1)
    finish(0)
    recon(core, 1, part)
    finish(1)

    mine = pl.ds(pl.multiple_of(512 * core + 128 * y + 32 * x, 32), 32)
    full = part[1, pl.ds(pl.multiple_of(128 + 32 * x, 32), 32), :]
    full = full + dec_bias[...] - cols[mine, :].astype(F32)
    for slot in range(1, 16):
        scatter[slot].wait_recv()
        full = full + rs_recv[slot].astype(F32)
    err[mine, :] = full.astype(BF16)

    gather = {}
    for dy, dx in PLANE:
        if dy or dx:
            slot = 4 * dy + dx
            gather[slot] = remote(err.at[mine], err.at[mine], sem_g, slot, in_plane(dy, dx))
            gather[slot].start()
    across = {}
    for dy in range(4):
        for dx in range(4):
            if dy or dx:
                gather[4 * dy + dx].wait_recv()
        rows = pl.ds(pl.multiple_of(512 * core + 128 * lax.rem(y + 4 - dy, 4), 128), 128)
        across[dy] = remote(err.at[rows], err.at[rows], sem_h, dy, sibling)
        across[dy].start()

    def code_grad(block):
        rows = pl.ds(pl.multiple_of(256 * block, 256), 256)
        grad_part[block] = jnp.zeros((64, 256), F32)

        @pl.loop(0, 4)
        def _(n):
            lats = pl.ds(pl.multiple_of(512 * n, 512), 512)
            scores = lax.dot_general(dec_v[lats, :], err[rows, :], NT, preferred_element_type=F32)
            where = key_t[:, rows]
            total = grad_part[block]
            for b in range(8):
                total += jnp.where(where == 8 * n + b, scores[64 * b:64 * b + 64, :], 0.0)
            grad_part[block] = total

    code_grad(2 * core)
    code_grad(2 * core + 1)
    for dy in range(4):
        across[dy].wait_recv()
    code_grad(2 * other)
    code_grad(2 * other + 1)

    grads = {}
    for o in ORDER:
        to = along(o)
        grads[o] = remote(grad_part.at[to], grad_recv.at[o], sem_d, o, (to, lat))
        grads[o].start()

    bias_out[...] = jnp.dot(jnp.ones((16, 1024), BF16), err[...], preferred_element_type=F32)[:8]

    def dec_rows(n):
        return pl.ds(pl.multiple_of(256 * n, 256), 256)

    def dec_grads(first, last):
        @pl.loop(first, last)
        def _(n):
            where, values = key_t[...], codes_t[...]
            wide = jnp.concatenate(
                [jnp.where(where == 4 * n + b, values, 0.0).astype(BF16) for b in range(4)], axis=0)
            dec_grad_v[dec_rows(n), :] = jnp.dot(wide, err[...], preferred_element_type=F32).astype(BF16)
            pltpu.make_async_copy(dec_grad_v.at[dec_rows(n)], dec_grad_out.at[dec_rows(n)], sem_o.at[n]).start()

    dec_grads(0, 4)
    total = grad_part[z]
    for o in ORDER:
        grads[o].wait_recv()
        total = total + grad_recv[o]
    grad_out[z] = total
    shares = {}
    for o in ORDER:
        shares[o] = remote(grad_out.at[z], grad_out.at[z], sem_e, o, (along(o), lat))
        shares[o].start()
    dec_grads(4, 8)

    for o in ORDER:
        shares[o].wait()
        for group in (sends, forwards, returns, spread_codes, grads):
            group[o].wait_send()
    for group in (to_sibling, scatter, gather, across):
        for copy in group.values():
            copy.wait_send()
    store_cols.wait()

    @pl.loop(0, 8)
    def _(n):
        pltpu.make_async_copy(dec_grad_v.at[dec_rows(n)], dec_grad_out.at[dec_rows(n)], sem_o.at[n]).wait()


def enc_grads(cols, grad, idx_t, lat_ref, dec_in, enc_out, enc_bias_out, dec_out, grad2, key, sem):
    n = pl.program_id(0)

    @pl.when(n == 0)
    def _():
        pltpu.make_async_copy(dec_in, dec_out, sem).start()
        odd = (lax.broadcasted_iota(I32, (128, 128), 1) >= 64).astype(I32)
        for g in range(8):
            piece = lax.shift_right_logical(idx_t[:, 128 * g:128 * g + 128], 6) - 32 * lat_ref[0]
            key[128 * g:128 * g + 128, :] = jnp.concatenate([piece, piece], axis=0).T - odd
            piece = grad[g // 2, :, 128 * (g % 2):128 * (g % 2) + 128]
            grad2[128 * g:128 * g + 128, :] = jnp.concatenate([piece, piece], axis=0).T

    where, values = key[...], grad2[...]
    wide = [jnp.where(where == 8 * n + 2 * j, values, 0.0) for j in range(4)]
    for j in range(4):
        enc_bias_out[:, 128 * j:128 * j + 128] = jnp.sum(wide[j], axis=0, keepdims=True)
    wide = jnp.concatenate([w.astype(BF16) for w in wide], axis=1)
    enc_out[...] = lax.dot_general(
        cols[...], wide, (((0,), (0,)), ((), ())), preferred_element_type=F32).astype(BF16)

    @pl.when(n == 3)
    def _():
        pltpu.make_async_copy(dec_in, dec_out, sem).wait()


def local(tokens, indices, enc_weight, dec_weight, enc_bias, dec_bias):
    idx_t = indices.T
    vmem = pl.BlockSpec(memory_space=pltpu.VMEM)
    hbm = pl.BlockSpec(memory_space=pl.ANY)
    dma = pltpu.SemaphoreType.DMA
    cols, dec_grad, grad, bias_grad = pl.pallas_call(
        exchange,
        out_shape=[
            jax.ShapeDtypeStruct((1024, 1024), BF16),
            jax.ShapeDtypeStruct((2048, 1024), BF16),
            jax.ShapeDtypeStruct((4, 64, 256), F32),
            jax.ShapeDtypeStruct((8, 1024), F32),
        ],
        in_specs=[hbm, vmem, hbm, hbm, vmem, vmem],
        out_specs=[hbm, hbm, vmem, vmem],
        scratch_shapes=[
            pltpu.VMEM((1024, 1024), BF16),
            pltpu.VMEM((1024, 2048), BF16),
            pltpu.VMEM((2048, 1024), BF16),
            pltpu.VMEM((1024, 128), I32),
            pltpu.VMEM((64, 1024), I32),
            pltpu.VMEM((256, 128), F32),
            pltpu.VMEM((128, 128), F32),
            pltpu.VMEM((4, 128, 128), F32),
            pltpu.VMEM((4, 128, 128), F32),
            pltpu.VMEM((4, 128, 128), BF16),
            pltpu.VMEM((1024, 128), F32),
            pltpu.VMEM((64, 1024), F32),
            pltpu.VMEM((256, 2048), BF16),
            pltpu.VMEM((2, 256, 1024), F32),
            pltpu.VMEM((2, 256, 1024), F32),
            pltpu.VMEM((2, 256, 1024), F32),
            pltpu.VMEM((2, 256, 1024), BF16),
            pltpu.VMEM((16, 32, 1024), BF16),
            pltpu.VMEM((1024, 1024), BF16),
            pltpu.VMEM((4, 64, 256), F32),
            pltpu.VMEM((4, 64, 256), F32),
            pltpu.VMEM((2048, 1024), BF16),
            dma((4,)), dma((2, 4)), dma((2, 4)), dma((2, 4)), dma((2, 4)), dma((2, 2)),
            dma((2, 16)), dma((2, 16)), dma((2, 4)), dma((2, 4)), dma((2, 4)), dma((8,)),
        ],
        compiler_params=pltpu.CompilerParams(
            collective_id=0, has_side_effects=True, vmem_limit_bytes=48 * 2**20),
        name="exchange",
    )(tokens, idx_t, enc_weight, dec_weight, enc_bias[None, :], dec_bias[None, :])

    enc_grad, enc_bias_grad, dec_grad = pl.pallas_call(
        enc_grads,
        grid=(4,),
        out_shape=[
            jax.ShapeDtypeStruct((1024, 2048), BF16),
            jax.ShapeDtypeStruct((1, 2048), F32),
            jax.ShapeDtypeStruct((2048, 1024), BF16),
        ],
        in_specs=[
            pl.BlockSpec((1024, 1024), lambda n: (0, 0)),
            pl.BlockSpec((4, 64, 256), lambda n: (0, 0, 0)),
            pl.BlockSpec((64, 1024), lambda n: (0, 0)),
            pl.BlockSpec(memory_space=pltpu.SMEM),
            hbm,
        ],
        out_specs=[
            pl.BlockSpec((1024, 512), lambda n: (0, n)),
            pl.BlockSpec((1, 512), lambda n: (0, n)),
            hbm,
        ],
        scratch_shapes=[pltpu.VMEM((1024, 128), F32), pltpu.VMEM((1024, 128), I32), dma(())],
        compiler_params=pltpu.CompilerParams(vmem_limit_bytes=48 * 2**20),
        name="enc_grads",
    )(cols, grad, idx_t, lax.axis_index("lat").reshape(1), dec_grad)
    return enc_grad, dec_grad, enc_bias_grad[0], bias_grad[0]


def solution(mesh):
    placed = (P("tok", None), P(), P("tok", "lat"), P("lat", "tok"), P("lat"), P("tok"))
    return jax.shard_map(
        local,
        mesh=mesh,
        in_specs=placed,
        out_specs=(P("tok", "lat"), P("lat", "tok"), P("lat"), P("tok")),
        check_vma=False,
    )
```

time: 290 us -> 226 us (0.78)
  Pallas kernels: 0 us -> 220 us
  waiting for transfers between devices: 204 us -> 0 us
  matrix products: 33.9 us -> 0 us
  local copies, waits for them, and re-layouts: 18.8 us -> 4.51 us
  between operations: 13.8 us -> 0.66 us
  other arithmetic: 13.1 us -> 0 us
  starting transfers between devices: 5.66 us -> 0 us
    pallas_call x0 -> x2, Pallas kernels: none -> 220 us  [the longest x1 129 us: local(): pl.pallas_call(enc_grads, grid=(4,), out_shape=[jax.ShapeDtypeStruct((102...]
    psum x3 -> x0, waiting for transfers between devices: 185 us -> none  [the longest x1 112 us: local(): recon_sum = lax.psum(partial_recon, 'lat')]
    dot_general x5 -> x0, matrix products: 33.9 us -> none  [the longest x1 9.41 us: local(): lax.dot_general(dense_codes, error_half, (((0,), (0,)), ((), ())), prefer...]
    all_to_all x1 -> x0, waiting for transfers between devices: 19.6 us -> none  [local(): lax.all_to_all(tokens, 'tok', split_axis=1, concat_axis=0, tiled=True)]
    unnamed x16 -> x8, local copies, waits for them, and re-layouts: 14.9 us -> 3.92 us
    reduce_sum x4 -> x0, other arithmetic: 8.37 us -> none  [the longest x1 3.79 us: local(): bias_grad = jnp.sum(error_full, axis=0)]
    all_to_all x1 -> x0, starting transfers between devices: 5.39 us -> none  [local(): lax.all_to_all(tokens, 'tok', split_axis=1, concat_axis=0, tiled=True)]
    convert_element_type x2 -> x0, other arithmetic: 3.32 us -> none  [the longest x1 2.2 us: local(): dense_grad.astype(jnp.bfloat16)]
  transfers between devices with their start and end apart: 4 -> 0, of which waited for: 4 -> 0; matrix products, arithmetic and copies ran while one was open for 6% -> 0% of each run, Pallas kernels for 0% -> 0%
where the time goes in v1:
time: 226 us; the launch traced here: 225 us
  Pallas kernels  220 us (97%)
  local copies, waits for them, and re-layouts  4.51 us (2%)
    pallas_call x1, Pallas kernels, local(): pl.pallas_call(enc_grads, grid=(4,), out_shape=[jax.ShapeDtypeStruct((102...  129 us
    pallas_call x1, Pallas kernels, local(): pl.pallas_call(exchange, out_shape=[jax.ShapeDtypeStruct((1024, 1024), BF...  90.6 us

profile of v1, /device:TPU:0, one launch (start us, length us, event | category | flops | bytes accessed | tf_op | source)
XLA Modules:
  0.0 224.9 jit_solution(10280031466946572512)
XLA Ops:
  0.6 0.0 copy-start
  0.6 1.6 copy-done
  2.2 0.0 copy-start.1
  2.2 0.9 copy-done.1
  3.2 0.0 copy-start.2
  3.2 0.7 copy-done.2
  3.9 0.0 copy-start.3
  3.9 0.7 copy-done.3
  4.6 90.6 %exchange.1 = (bf16[1024,1024]{1,0:T(8,128)(2,1)S(1)}, bf16[2048,1024]{1,0:T(8,128)(2,1)}, f32[4,64,256]{2,1,0:T(8,128)S(1)}, f32[8,1024]{1,0:T(8,128)S(1)}) custom-call(bf16[256,4096]{1,0:T(8,128)(2,1)S(1)} %copy-done, s32[64,1024]{1,0:T(8,128)S(1)} %bitcast.6, bf16[1024,2048]{1,0:T(8,128)(2,1)} %enc.1, bf16[2048,1024]{1,0:T(8,128)(2,1)} %dec.1, ...), custom_call_target="tpu_custom_call" | custom-call | tf_op jit(solution)/shard_map/exchange/pallas_call | solution.py:324
  95.1 0.6 slice.3
  95.7 129.1 %enc_grads.1 = (bf16[1024,2048]{1,0:T(8,128)(2,1)}, f32[1,2048]{1,0:T(1,128)}, bf16[2048,1024]{1,0:T(8,128)(2,1)}) custom-call(bf16[1024,1024]{1,0:T(8,128)(2,1)S(1)} %get-tuple-element.11.cols, f32[4,64,256]{2,1,0:T(8,128)S(1)} %get-tuple-element.12.grad, s32[64,1024]{1,0:T(8,128)S(1)} %bitcast.7, s32[1]{0:T(128)} %bitcast.3.lat_ref, ...), custom_call_target="tpu_custom_call" | custom-call | tf_op jit(solution)/shard_map/enc_grads/pallas_call | solution.py:365
Async XLA Ops:
  0.6 1.6 copy-start
  2.2 0.9 copy-start.1
  3.2 0.7 copy-start.2
  3.9 0.7 copy-start.3

commit v2 on v1

--- a/solution.py
+++ b/solution.py
@@ -290,12 +290,11 @@
         pltpu.make_async_copy(dec_grad_v.at[dec_rows(n)], dec_grad_out.at[dec_rows(n)], sem_o.at[n]).wait()
 
 
-def enc_grads(cols, grad, idx_t, lat_ref, dec_in, enc_out, enc_bias_out, dec_out, grad2, key, sem):
+def enc_grads(cols, grad, idx_t, lat_ref, dec_in, enc_out, enc_bias_out, dec_out, grad2, key):
     n = pl.program_id(0)
 
     @pl.when(n == 0)
     def _():
-        pltpu.make_async_copy(dec_in, dec_out, sem).start()
         odd = (lax.broadcasted_iota(I32, (128, 128), 1) >= 64).astype(I32)
         for g in range(8):
             piece = lax.shift_right_logical(idx_t[:, 128 * g:128 * g + 128], 6) - 32 * lat_ref[0]
@@ -310,10 +309,7 @@
     wide = jnp.concatenate([w.astype(BF16) for w in wide], axis=1)
     enc_out[...] = lax.dot_general(
         cols[...], wide, (((0,), (0,)), ((), ())), preferred_element_type=F32).astype(BF16)
-
-    @pl.when(n == 3)
-    def _():
-        pltpu.make_async_copy(dec_in, dec_out, sem).wait()
+    dec_out[...] = dec_in[...]
 
 
 def local(tokens, indices, enc_weight, dec_weight, enc_bias, dec_bias):
@@ -375,14 +371,14 @@
             pl.BlockSpec((4, 64, 256), lambda n: (0, 0, 0)),
             pl.BlockSpec((64, 1024), lambda n: (0, 0)),
             pl.BlockSpec(memory_space=pltpu.SMEM),
-            hbm,
+            pl.BlockSpec((512, 1024), lambda n: (n, 0)),
         ],
         out_specs=[
             pl.BlockSpec((1024, 512), lambda n: (0, n)),
             pl.BlockSpec((1, 512), lambda n: (0, n)),
-            hbm,
-        ],
-        scratch_shapes=[pltpu.VMEM((1024, 128), F32), pltpu.VMEM((1024, 128), I32), dma(())],
+            pl.BlockSpec((512, 1024), lambda n: (n, 0)),
+        ],
+        scratch_shapes=[pltpu.VMEM((1024, 128), F32), pltpu.VMEM((1024, 128), I32)],
         compiler_params=pltpu.CompilerParams(vmem_limit_bytes=48 * 2**20),
         name="enc_grads",
     )(cols, grad, idx_t, lax.axis_index("lat").reshape(1), dec_grad)

time: 226 us -> 106 us (0.47)
  Pallas kernels: 220 us -> 99.4 us
    pallas_call x1, Pallas kernels: 129 us -> 8.89 us  [local(): pl.pallas_call(enc_grads, grid=(4,), out_shape=[jax.ShapeDtypeStruct((102...]
where the time goes in v2:
time: 106 us; the launch traced here: 105 us
  Pallas kernels  99.4 us (94%)
  local copies, waits for them, and re-layouts  4.51 us (4%)
    pallas_call x1, Pallas kernels, local(): pl.pallas_call(exchange, out_shape=[jax.ShapeDtypeStruct((1024, 1024), BF...  90.6 us
    pallas_call x1, Pallas kernels, local(): pl.pallas_call(enc_grads, grid=(4,), out_shape=[jax.ShapeDtypeStruct((102...  8.89 us
    unnamed x8, local copies, waits for them, and re-layouts  3.92 us

profile of v2, /device:TPU:0, one launch (start us, length us, event | category | flops | bytes accessed | tf_op | source)
XLA Modules:
  0.0 104.6 jit_solution(2414234112681772898)
XLA Ops:
  0.6 0.0 copy-start
  0.6 1.6 %copy-done = bf16[256,4096]{1,0:T(8,128)(2,1)S(1)} copy-done((bf16[256,4096]{1,0:T(8,128)(2,1)S(1)}, bf16[256,4096]{1,0:T(8,128)(2,1)}, u32[]{:S(2)}) %copy-start) | copy-done | bytes 2097176
  2.2 0.0 copy-start.1
  2.2 0.9 copy-done.1
  3.2 0.0 copy-start.2
  3.2 0.7 copy-done.2
  3.9 0.0 copy-start.3
  3.9 0.7 copy-done.3
  4.6 90.6 %exchange.1 = (bf16[1024,1024]{1,0:T(8,128)(2,1)S(1)}, bf16[2048,1024]{1,0:T(8,128)(2,1)}, f32[4,64,256]{2,1,0:T(8,128)S(1)}, f32[8,1024]{1,0:T(8,128)S(1)}) custom-call(bf16[256,4096]{1,0:T(8,128)(2,1)S(1)} %copy-done, s32[64,1024]{1,0:T(8,128)S(1)} %bitcast.6, bf16[1024,2048]{1,0:T(8,128)(2,1)} %enc.1, bf16[2048,1024]{1,0:T(8,128)(2,1)} %dec.1, ...), custom_call_target="tpu_custom_call" | custom-call | tf_op jit(solution)/shard_map/exchange/pallas_call | solution.py:320
  95.1 0.6 slice.3
  95.7 8.9 %enc_grads.1 = (bf16[1024,2048]{1,0:T(8,128)(2,1)}, f32[1,2048]{1,0:T(1,128)}, bf16[2048,1024]{1,0:T(8,128)(2,1)}) custom-call(bf16[1024,1024]{1,0:T(8,128)(2,1)S(1)} %get-tuple-element.11.cols, f32[4,64,256]{2,1,0:T(8,128)S(1)} %get-tuple-element.12.grad, s32[64,1024]{1,0:T(8,128)S(1)} %bitcast.7, s32[1]{0:T(128)} %bitcast.3.lat_ref, ...), custom_call_target="tpu_custom_call" | custom-call | tf_op jit(solution)/shard_map/enc_grads/pallas_call | solution.py:361
Async XLA Ops:
  0.6 1.6 %copy-start = (bf16[256,4096]{1,0:T(8,128)(2,1)S(1)}, bf16[256,4096]{1,0:T(8,128)(2,1)}, u32[]{:S(2)}) copy-start(bf16[256,4096]{1,0:T(8,128)(2,1)} %tokens.1) | copy-start | bytes 6291460
  2.2 0.9 copy-start.1
  3.2 0.7 copy-start.2
  3.9 0.7 copy-start.3

commit v3 on v2

v3 whole, which is shorter than its diff:
```python
import jax
import jax.numpy as jnp
from jax import lax
from jax.experimental import pallas as pl
from jax.experimental.pallas import tpu as pltpu
from jax.sharding import PartitionSpec as P

MESH = pl.DeviceIdType.MESH
F32, BF16, I32 = jnp.float32, jnp.bfloat16, jnp.int32
NT = (((1,), (1,)), ((), ()))
PLANE = tuple((dy, dx) for dy in range(4) for dx in range(4))
ORDER = (1, 3, 2)


def exchange(
    tokens, idx_in, enc, dec, enc_bias, dec_bias,
    cols_out, dec_grad_out, grad_out, bias_out,
    idx_t, bias_e, bias_d, cols, enc2, dec2, key, key_t, picked, own_pre, pre_send, pre_recv,
    codes, dense, part, rs_send, rs_recv, err, grad_part, grad_recv, dec_grad_v,
    sem_local, sem_a, sem_w, sem_f, sem_b, sem_c, sem_k, sem_r, sem_g, sem_h, sem_d, sem_e, sem_o,
):
    z, lat = lax.axis_index("tok"), lax.axis_index("lat")
    y, x, core = lat // 8, (lat // 2) % 4, lat % 2
    other = 1 - core
    sib_lat = lat + 1 - 2 * core
    sibling = (z, sib_lat)

    def along(offset):
        return lax.rem(z + offset, 4)

    def in_plane(dy, dx):
        return (z, lax.rem(y + dy, 4) * 8 + lax.rem(x + dx, 4) * 2 + core)

    def remote(src, dst, sems, index, device):
        return pltpu.make_async_remote_copy(
            src_ref=src, dst_ref=dst, send_sem=sems.at[0, index], recv_sem=sems.at[1, index],
            device_id=device, device_id_type=MESH,
        )

    barrier = pltpu.get_barrier_semaphore()
    peers = [(along(o), lat) for o in ORDER] + [sibling]
    peers += [(along(o), sib_lat) for o in ORDER]
    peers += [in_plane(dy, dx) for dy, dx in PLANE if dy or dx]
    for peer in peers:
        pl.semaphore_signal(barrier, inc=1, device_id=peer, device_id_type=MESH)

    enc_rows = pl.ds(pl.multiple_of(1024 * core, 1024), 1024)
    dec_rows = pl.ds(pl.multiple_of(2048 * core, 2048), 2048)
    loads = [
        pltpu.make_async_copy(
            tokens.at[:, pl.ds(pl.multiple_of(1024 * z, 1024), 1024)],
            cols.at[pl.ds(pl.multiple_of(256 * z, 256), 256)], sem_local.at[0]),
        pltpu.make_async_copy(idx_in, idx_t, sem_local.at[1]),
        pltpu.make_async_copy(enc_bias, bias_e.at[core], sem_local.at[2]),
        pltpu.make_async_copy(enc, enc2.at[enc_rows], sem_local.at[3]),
        pltpu.make_async_copy(dec_bias, bias_d, sem_local.at[4]),
        pltpu.make_async_copy(dec, dec2.at[dec_rows], sem_local.at[5]),
    ]
    for copy in loads:
        copy.start()

    pl.semaphore_wait(barrier, len(peers))

    def half(block, which):
        return pl.ds(pl.multiple_of(256 * block + 128 * which, 128), 128)

    sends = {}
    for o in ORDER:
        to = along(o)
        sends[o] = remote(
            tokens.at[pl.ds(pl.multiple_of(128 * core, 128), 128), pl.ds(pl.multiple_of(1024 * to, 1024), 1024)],
            cols.at[half(z, core)], sem_a, o, (to, lat))
        sends[o].start()
    give_bias = remote(enc_bias, bias_e.at[core], sem_w, 0, sibling)
    give_enc = remote(enc, enc2.at[enc_rows], sem_w, 1, sibling)
    give_dec = remote(dec, dec2.at[dec_rows], sem_w, 2, sibling)
    give_bias.start()
    give_enc.start()

    loads[1].wait()
    odd = (lax.broadcasted_iota(I32, (128, 128), 1) >= 64).astype(I32)
    for g in range(4):
        for h in range(2):
            at = 256 * g + 128 * h
            band = lax.shift_right_logical(idx_t[:, at:at + 128], 6) - 64 * (lat // 2)
            key_t[:, 512 * h + 128 * g:512 * h + 128 * g + 128] = band
        band = lax.shift_right_logical(idx_t[:, half(g, core)], 6) - 64 * (lat // 2)
        key[g] = jnp.concatenate([band, band], axis=0).T - odd

    def pick(blocks, which, bias_first):
        rows = jnp.concatenate([cols[half(b, core), :] for b in blocks], axis=0) if len(blocks) > 1 else cols[half(blocks[0], core), :]
        weights = pl.ds(pl.multiple_of(1024 * which, 1024), 1024)

        @pl.loop(0, 4)
        def _(n):
            base = pl.multiple_of(512 * n, 512)
            scores = jnp.dot(rows, enc2[weights, pl.ds(base, 512)], preferred_element_type=F32)
            if bias_first:
                scores = scores + bias_e[which, :, pl.ds(base, 512)]
            for i, b in enumerate(blocks):
                where = key[b]
                total = picked[b]
                for j in range(4):
                    total += jnp.where(
                        where == 32 * which + 8 * n + 2 * j,
                        scores[128 * i:128 * i + 128, 128 * j:128 * j + 128], 0.0)
                picked[b] = total

    def folded(block):
        turned = picked[block].T
        return turned[:64] + turned[64:]

    picked[...] = jnp.zeros_like(picked)
    loads[0].wait()
    loads[2].wait()
    loads[3].wait()
    pick([z], core, True)

    returns = {}
    forwards = {}

    def forward(o):
        rows = half(along(4 - o), core)
        forwards[o] = remote(cols.at[rows], cols.at[rows], sem_f, o, sibling)
        forwards[o].start()

    def give_back(o):
        pre_send[o] = folded(along(4 - o))
        returns[o] = remote(pre_send.at[o], pre_recv.at[o], sem_b, o, (along(4 - o), lat))
        returns[o].start()

    give_bias.wait_recv()
    give_enc.wait_recv()
    give_enc.wait_send()
    give_dec.start()
    pick([z], other, True)
    own_pre[...] = folded(z)
    sends[1].wait_recv()
    sends[3].wait_recv()
    pair = [along(3), along(1)]
    pick(pair, core, False)
    pick(pair, other, False)
    give_back(1)
    give_back(3)
    sends[2].wait_recv()
    last = [along(2)]
    pick(last, core, False)
    pick(last, other, False)
    give_back(2)
    for o in ORDER:
        forward(o)

    total = own_pre[...]
    for o in ORDER:
        returns[o].wait_recv()
        total = total + pre_recv[o]
    codes[core, z] = total.astype(BF16)
    shared = {}
    for o in ORDER:
        shared[o] = remote(codes.at[core, z], codes.at[core, z], sem_c, o, (along(o), lat))
        shared[o].start()
    for copy in loads[4:]:
        copy.wait()
    give_dec.wait_recv()
    for o in ORDER:
        shared[o].wait_recv()
    swap_codes = remote(codes.at[core], codes.at[core], sem_k, 0, sibling)
    swap_codes.start()

    scatter = {}

    def recon(chunk):
        groups = [lax.rem(y + (1 + 2 * chunk + pos) % 4, 4) for pos in range(2)]
        for pos in range(2):
            turned = codes[core, groups[pos]].astype(F32)
            values = jnp.concatenate([turned, turned], axis=0).T
            where = key[groups[pos]]
            for j in range(32):
                dense[128 * pos:128 * pos + 128, 128 * j:128 * j + 128] = jnp.where(
                    where == 2 * j, values, 0.0).astype(BF16)

        @pl.loop(0, 2)
        def _(n):
            base = pl.ds(pl.multiple_of(512 * n, 512), 512)
            out = jnp.dot(dense[...], dec2[:, base], preferred_element_type=F32)
            if chunk == 1:
                part[:, base] = out[128:]
            rs_send[chunk, :, base] = out.astype(BF16)

        for pos in range(2):
            dy = (1 + 2 * chunk + pos) % 4
            for dx in range(4):
                if dy == 0 and dx == 0:
                    continue
                slot = 4 * dy + dx
                rows = pl.ds(pl.multiple_of(128 * pos + 32 * lax.rem(x + dx, 4), 32), 32)
                scatter[slot] = remote(rs_send.at[chunk, rows], rs_recv.at[slot], sem_r, slot, in_plane(dy, dx))
                scatter[slot].start()

    recon(0)
    recon(1)

    mine = pl.ds(pl.multiple_of(32 * x, 32), 32)
    full = part[mine, :] + bias_d[...]
    full = full - cols[pl.ds(pl.multiple_of(256 * y + 128 * core + 32 * x, 32), 32), :].astype(F32)
    for slot in range(1, 16):
        scatter[slot].wait_recv()
        full = full + rs_recv[slot].astype(F32)
    err[core, y, mine, :] = full.astype(BF16)

    gather = {}
    for dy, dx in PLANE:
        if dy or dx:
            slot = 4 * dy + dx
            gather[slot] = remote(
                err.at[core, y, mine], err.at[core, y, mine], sem_g, slot, in_plane(dy, dx))
            gather[slot].start()

    across = {}

    def code_grad(dys):
        groups = []
        for dy in dys:
            for dx in range(4):
                if dy or dx:
                    gather[4 * dy + dx].wait_recv()
            group = lax.rem(y + 4 - dy, 4)
            across[dy] = remote(err.at[core, group], err.at[core, group], sem_h, dy, sibling)
            across[dy].start()
            groups.append(group)
        rows = jnp.concatenate([err[core, g] for g in groups], axis=0)
        for g in groups:
            grad_part[g] = jnp.zeros((64, 128), F32)

        @pl.loop(0, 8)
        def _(n):
            lats = pl.ds(pl.multiple_of(512 * n, 512), 512)
            scores = lax.dot_general(dec2[lats, :], rows, NT, preferred_element_type=F32)
            for i, g in enumerate(groups):
                where = key_t[:, pl.ds(pl.multiple_of(512 * core + 128 * g, 128), 128)]
                total = grad_part[g]
                for b in range(8):
                    total += jnp.where(
                        where == 8 * n + b, scores[64 * b:64 * b + 64, 128 * i:128 * i + 128], 0.0)
                grad_part[g] = total

    code_grad((0, 1))
    code_grad((2, 3))

    grads = {}
    for o in ORDER:
        to = along(o)
        grads[o] = remote(grad_part.at[to], grad_recv.at[o], sem_d, o, (to, lat))
        grads[o].start()

    swap_codes.wait_recv()
    for dy in range(4):
        across[dy].wait_recv()

    def tile(n):
        return pl.ds(pl.multiple_of(256 * n, 256), 256)

    def dec_grads(first, last):
        values = jnp.concatenate(
            [codes[h, g].astype(F32) for h in range(2) for g in range(4)], axis=1)
        errors = err[...].reshape(1024, 1024)

        @pl.loop(first, last)
        def _(n):
            where = key_t[...]
            wide = jnp.concatenate(
                [jnp.where(where == 32 * core + 4 * n + b, values, 0.0).astype(BF16) for b in range(4)], axis=0)
            dec_grad_v[tile(n), :] = jnp.dot(wide, errors, preferred_element_type=F32).astype(BF16)
            pltpu.make_async_copy(dec_grad_v.at[tile(n)], dec_grad_out.at[tile(n)], sem_o.at[n]).start()

    for o in ORDER:
        forwards[o].wait_recv()
    store_cols = pltpu.make_async_copy(cols, cols_out, sem_local.at[6])
    store_cols.start()
    dec_grads(0, 4)
    total = grad_part[z]
    for o in ORDER:
        grads[o].wait_recv()
        total = total + grad_recv[o]
    grad_out[core, z] = total
    shares = []
    for o in (0,) + ORDER:
        if o:
            shares.append(remote(grad_out.at[core, z], grad_out.at[core, z], sem_e, o, (along(o), lat)))
            shares[-1].start()
        shares.append(remote(grad_out.at[core, z], grad_out.at[core, z], sem_e, 4 + o, (along(o), sib_lat)))
        shares[-1].start()
    dec_grads(4, 8)
    bias_out[...] = jnp.dot(
        jnp.ones((16, 1024), BF16), err[...].reshape(1024, 1024), preferred_element_type=F32)[:1]

    for copy in shares:
        copy.wait()
    for o in ORDER:
        for group in (sends, forwards, returns, shared, grads):
            group[o].wait_send()
    for copy in [give_bias, give_dec, swap_codes] + list(scatter.values()) + list(gather.values()) + list(across.values()):
        copy.wait_send()
    store_cols.wait()

    @pl.loop(0, 8)
    def _(n):
        pltpu.make_async_copy(dec_grad_v.at[tile(n)], dec_grad_out.at[tile(n)], sem_o.at[n]).wait()


def enc_grads(cols, grad, idx_t, lat_ref, dec_in, enc_out, enc_bias_out, dec_out, grad2, key):
    n = pl.program_id(0)

    @pl.when(n == 0)
    def _():
        odd = (lax.broadcasted_iota(I32, (128, 128), 1) >= 64).astype(I32)
        for g in range(8):
            piece = lax.shift_right_logical(idx_t[:, 128 * g:128 * g + 128], 6) - 32 * lat_ref[0]
            key[128 * g:128 * g + 128, :] = jnp.concatenate([piece, piece], axis=0).T - odd
            piece = grad[g % 2, g // 2]
            grad2[128 * g:128 * g + 128, :] = jnp.concatenate([piece, piece], axis=0).T

    where, values = key[...], grad2[...]
    wide = [jnp.where(where == 8 * n + 2 * j, values, 0.0) for j in range(4)]
    for j in range(4):
        enc_bias_out[:, 128 * j:128 * j + 128] = jnp.sum(wide[j], axis=0, keepdims=True)
    wide = jnp.concatenate([w.astype(BF16) for w in wide], axis=1)
    enc_out[...] = lax.dot_general(
        cols[...], wide, (((0,), (0,)), ((), ())), preferred_element_type=F32).astype(BF16)
    dec_out[...] = dec_in[...]


def local(tokens, indices, enc_weight, dec_weight, enc_bias, dec_bias):
    idx_t = indices.T
    vmem = pl.BlockSpec(memory_space=pltpu.VMEM)
    hbm = pl.BlockSpec(memory_space=pl.ANY)
    dma = pltpu.SemaphoreType.DMA
    cols, dec_grad, grad, bias_grad = pl.pallas_call(
        exchange,
        out_shape=[
            jax.ShapeDtypeStruct((1024, 1024), BF16),
            jax.ShapeDtypeStruct((2048, 1024), BF16),
            jax.ShapeDtypeStruct((2, 4, 64, 128), F32),
            jax.ShapeDtypeStruct((1, 1024), F32),
        ],
        in_specs=[hbm] * 6,
        out_specs=[hbm, hbm, vmem, vmem],
        scratch_shapes=[
            pltpu.VMEM((64, 1024), I32),
            pltpu.VMEM((2, 1, 2048), F32),
            pltpu.VMEM((1, 1024), F32),
            pltpu.VMEM((1024, 1024), BF16),
            pltpu.VMEM((2048, 2048), BF16),
            pltpu.VMEM((4096, 1024), BF16),
            pltpu.VMEM((4, 128, 128), I32),
            pltpu.VMEM((64, 1024), I32),
            pltpu.VMEM((4, 128, 128), F32),
            pltpu.VMEM((64, 128), F32),
            pltpu.VMEM((4, 64, 128), F32),
            pltpu.VMEM((4, 64, 128), F32),
            pltpu.VMEM((2, 4, 64, 128), BF16),
            pltpu.VMEM((256, 4096), BF16),
            pltpu.VMEM((128, 1024), F32),
            pltpu.VMEM((2, 256, 1024), BF16),
            pltpu.VMEM((16, 32, 1024), BF16),
            pltpu.VMEM((2, 4, 128, 1024), BF16),
            pltpu.VMEM((4, 64, 128), F32),
            pltpu.VMEM((4, 64, 128), F32),
            pltpu.VMEM((2048, 1024), BF16),
            dma((7,)), dma((2, 4)), dma((2, 3)), dma((2, 4)), dma((2, 4)), dma((2, 4)), dma((2, 1)),
            dma((2, 16)), dma((2, 16)), dma((2, 4)), dma((2, 4)), dma((2, 8)), dma((8,)),
        ],
        compiler_params=pltpu.CompilerParams(
            collective_id=0, has_side_effects=True, vmem_limit_bytes=58 * 2**20),
        name="exchange",
    )(tokens, idx_t, enc_weight, dec_weight, enc_bias[None, :], dec_bias[None, :])

    enc_grad, enc_bias_grad, dec_grad = pl.pallas_call(
        enc_grads,
        grid=(4,),
        out_shape=[
            jax.ShapeDtypeStruct((1024, 2048), BF16),
            jax.ShapeDtypeStruct((1, 2048), F32),
            jax.ShapeDtypeStruct((2048, 1024), BF16),
        ],
        in_specs=[
            pl.BlockSpec((1024, 1024), lambda n: (0, 0)),
            pl.BlockSpec((2, 4, 64, 128), lambda n: (0, 0, 0, 0)),
            pl.BlockSpec((64, 1024), lambda n: (0, 0)),
            pl.BlockSpec(memory_space=pltpu.SMEM),
            pl.BlockSpec((512, 1024), lambda n: (n, 0)),
        ],
        out_specs=[
            pl.BlockSpec((1024, 512), lambda n: (0, n)),
            pl.BlockSpec((1, 512), lambda n: (0, n)),
            pl.BlockSpec((512, 1024), lambda n: (n, 0)),
        ],
        scratch_shapes=[pltpu.VMEM((1024, 128), F32), pltpu.VMEM((1024, 128), I32)],
        compiler_params=pltpu.CompilerParams(vmem_limit_bytes=58 * 2**20),
        name="enc_grads",
    )(cols, grad, idx_t, lax.axis_index("lat").reshape(1), dec_grad)
    return enc_grad, dec_grad, enc_bias_grad[0], bias_grad[0]


def solution(mesh):
    placed = (P("tok", None), P(), P("tok", "lat"), P("lat", "tok"), P("lat"), P("tok"))
    return jax.shard_map(
        local,
        mesh=mesh,
        in_specs=placed,
        out_specs=(P("tok", "lat"), P("lat", "tok"), P("lat"), P("tok")),
        check_vma=False,
    )
```

time: 106 us -> 89.9 us (0.85)
  Pallas kernels: 99.4 us -> 87.4 us
  local copies, waits for them, and re-layouts: 4.51 us -> 0.6 us
    pallas_call x1, Pallas kernels: 90.6 us -> 77.7 us  [local(): pl.pallas_call(exchange, out_shape=[jax.ShapeDtypeStruct((1024, 1024), BF...]
    unnamed x8 -> x3, local copies, waits for them, and re-layouts: 3.92 us -> 0.6 us
where the time goes in v3:
time: 89.9 us; the launch traced here: 88.6 us
  Pallas kernels  87.4 us (97%)
    pallas_call x1, Pallas kernels, local(): pl.pallas_call(exchange, out_shape=[jax.ShapeDtypeStruct((1024, 1024), BF...  77.7 us
    pallas_call x1, Pallas kernels, local(): pl.pallas_call(enc_grads, grid=(4,), out_shape=[jax.ShapeDtypeStruct((102...  9.68 us

profile of v3, /device:TPU:0, one launch (start us, length us, event | category | flops | bytes accessed | tf_op | source)
XLA Modules:
  0.0 88.6 jit_solution(9248243467811730801)
XLA Ops:
  0.6 77.7 %exchange.1 = (bf16[1024,1024]{1,0:T(8,128)(2,1)}, bf16[2048,1024]{1,0:T(8,128)(2,1)}, f32[2,4,64,128]{3,2,1,0:T(8,128)}, f32[1,1024]{1,0:T(1,128)}) custom-call(bf16[256,4096]{1,0:T(8,128)(2,1)} %tokens.1, s32[64,1024]{1,0:T(8,128)} %bitcast.6, bf16[1024,2048]{1,0:T(8,128)(2,1)} %enc.1, bf16[2048,1024]{1,0:T(8,128)(2,1)} %dec.1, f32[1,2048]{1,0:T(1,128)} %bitcast.8, ...), custom_call_target="tpu_custom_call" | custom-call | tf_op jit(solution)/shard_map/exchange/pallas_call | solution.py:338
  78.3 0.0 copy-start
  78.3 9.7 %enc_grads.1 = (bf16[1024,2048]{1,0:T(8,128)(2,1)}, f32[1,2048]{1,0:T(1,128)}, bf16[2048,1024]{1,0:T(8,128)(2,1)}) custom-call(bf16[1024,1024]{1,0:T(8,128)(2,1)} %get-tuple-element.11.cols, f32[2,4,64,128]{3,2,1,0:T(8,128)} %get-tuple-element.12.grad, s32[64,1024]{1,0:T(8,128)} %bitcast.7, s32[1]{0:T(128)} %bitcast.3.lat_ref, ...), custom_call_target="tpu_custom_call" | custom-call | tf_op jit(solution)/shard_map/enc_grads/pallas_call | solution.py:378
  88.0 0.0 copy-done
  88.0 0.6 copy.11
Async XLA Ops:
  78.3 9.7 %copy-start = (f32[1,1024]{1,0:T(1,128)S(1)}, f32[1,1024]{1,0:T(1,128)}, u32[]{:S(2)}) copy-start(f32[1,1024]{1,0:T(1,128)} %get-tuple-element.17) | copy-start | bytes 12292

commit v4 on v3

--- a/solution.py
+++ b/solution.py
@@ -16,7 +16,7 @@
     tokens, idx_in, enc, dec, enc_bias, dec_bias,
     cols_out, dec_grad_out, grad_out, bias_out,
     idx_t, bias_e, bias_d, cols, enc2, dec2, key, key_t, picked, own_pre, pre_send, pre_recv,
-    codes, dense, part, rs_send, rs_recv, err, grad_part, grad_recv, dec_grad_v,
+    codes, dense, cols_t, rs_send, rs_recv, err, grad_part, grad_recv, dec_grad_v,
     sem_local, sem_a, sem_w, sem_f, sem_b, sem_c, sem_k, sem_r, sem_g, sem_h, sem_d, sem_e, sem_o,
 ):
     z, lat = lax.axis_index("tok"), lax.axis_index("lat")
@@ -70,7 +70,8 @@
         sends[o] = remote(
             tokens.at[pl.ds(pl.multiple_of(128 * core, 128), 128), pl.ds(pl.multiple_of(1024 * to, 1024), 1024)],
             cols.at[half(z, core)], sem_a, o, (to, lat))
-        sends[o].start()
+        if o != 2:
+            sends[o].start()
     give_bias = remote(enc_bias, bias_e.at[core], sem_w, 0, sibling)
     give_enc = remote(enc, enc2.at[enc_rows], sem_w, 1, sibling)
     give_dec = remote(dec, dec2.at[dec_rows], sem_w, 2, sibling)
@@ -91,7 +92,7 @@
         rows = jnp.concatenate([cols[half(b, core), :] for b in blocks], axis=0) if len(blocks) > 1 else cols[half(blocks[0], core), :]
         weights = pl.ds(pl.multiple_of(1024 * which, 1024), 1024)
 
-        @pl.loop(0, 4)
+        @pl.loop(0, 4, unroll=True)
         def _(n):
             base = pl.multiple_of(512 * n, 512)
             scores = jnp.dot(rows, enc2[weights, pl.ds(base, 512)], preferred_element_type=F32)
@@ -129,19 +130,21 @@
         returns[o] = remote(pre_send.at[o], pre_recv.at[o], sem_b, o, (along(4 - o), lat))
         returns[o].start()
 
-    give_bias.wait_recv()
-    give_enc.wait_recv()
-    give_enc.wait_send()
-    give_dec.start()
-    pick([z], other, True)
-    own_pre[...] = folded(z)
+    sends[1].wait_send()
+    sends[3].wait_send()
+    sends[2].start()
     sends[1].wait_recv()
     sends[3].wait_recv()
     pair = [along(3), along(1)]
     pick(pair, core, False)
+    give_bias.wait_recv()
+    give_enc.wait()
+    give_dec.start()
     pick(pair, other, False)
     give_back(1)
     give_back(3)
+    pick([z], other, True)
+    own_pre[...] = folded(z)
     sends[2].wait_recv()
     last = [along(2)]
     pick(last, core, False)
@@ -167,75 +170,65 @@
     swap_codes = remote(codes.at[core], codes.at[core], sem_k, 0, sibling)
     swap_codes.start()
 
-    scatter = {}
+    spot = 4 * y + x
+    scatter, gather, across = {}, {}, {}
+
+    def share(chunk, place):
+        return pl.ds(pl.multiple_of(256 * chunk + 16 * place, 16), 16)
+
+    def partners(chunk):
+        for slot in range(1, 16):
+            dy, dx = PLANE[slot]
+            place = 4 * lax.rem(y + dy, 4) + lax.rem(x + dx, 4)
+            yield 16 * chunk + slot, place, in_plane(dy, dx)
 
     def recon(chunk):
-        groups = [lax.rem(y + (1 + 2 * chunk + pos) % 4, 4) for pos in range(2)]
         for pos in range(2):
-            turned = codes[core, groups[pos]].astype(F32)
+            turned = codes[core, 2 * chunk + pos].astype(F32)
             values = jnp.concatenate([turned, turned], axis=0).T
-            where = key[groups[pos]]
+            where = key[2 * chunk + pos]
             for j in range(32):
                 dense[128 * pos:128 * pos + 128, 128 * j:128 * j + 128] = jnp.where(
                     where == 2 * j, values, 0.0).astype(BF16)
 
-        @pl.loop(0, 2)
+        @pl.loop(0, 2, unroll=True)
         def _(n):
             base = pl.ds(pl.multiple_of(512 * n, 512), 512)
-            out = jnp.dot(dense[...], dec2[:, base], preferred_element_type=F32)
-            if chunk == 1:
-                part[:, base] = out[128:]
-            rs_send[chunk, :, base] = out.astype(BF16)
-
-        for pos in range(2):
-            dy = (1 + 2 * chunk + pos) % 4
-            for dx in range(4):
-                if dy == 0 and dx == 0:
-                    continue
-                slot = 4 * dy + dx
-                rows = pl.ds(pl.multiple_of(128 * pos + 32 * lax.rem(x + dx, 4), 32), 32)
-                scatter[slot] = remote(rs_send.at[chunk, rows], rs_recv.at[slot], sem_r, slot, in_plane(dy, dx))
-                scatter[slot].start()
-
-    recon(0)
-    recon(1)
-
-    mine = pl.ds(pl.multiple_of(32 * x, 32), 32)
-    full = part[mine, :] + bias_d[...]
-    full = full - cols[pl.ds(pl.multiple_of(256 * y + 128 * core + 32 * x, 32), 32), :].astype(F32)
-    for slot in range(1, 16):
-        scatter[slot].wait_recv()
-        full = full + rs_recv[slot].astype(F32)
-    err[core, y, mine, :] = full.astype(BF16)
-
-    gather = {}
-    for dy, dx in PLANE:
-        if dy or dx:
-            slot = 4 * dy + dx
-            gather[slot] = remote(
-                err.at[core, y, mine], err.at[core, y, mine], sem_g, slot, in_plane(dy, dx))
+            rs_send[256 * chunk:256 * chunk + 256, base] = jnp.dot(
+                dense[...], dec2[:, base], preferred_element_type=F32).astype(BF16)
+
+        for slot, place, device in partners(chunk):
+            scatter[slot] = remote(rs_send.at[share(chunk, place)], rs_recv.at[slot], sem_r, slot, device)
+            scatter[slot].start()
+
+    def error(chunk):
+        mine = share(chunk, spot)
+        rows = pl.ds(pl.multiple_of(512 * chunk + 256 * (spot // 8) + 128 * core + 16 * lax.rem(spot, 8), 16), 16)
+        full = rs_send[mine, :].astype(F32) + bias_d[...]
+        full = full - cols[rows, :].astype(F32)
+        for slot in range(16 * chunk + 1, 16 * chunk + 16):
+            scatter[slot].wait_recv()
+            full = full + rs_recv[slot].astype(F32)
+        err[core, mine, :] = full.astype(BF16)
+        for slot, _, device in partners(chunk):
+            gather[slot] = remote(err.at[core, mine], err.at[core, mine], sem_g, slot, device)
             gather[slot].start()
 
-    across = {}
-
-    def code_grad(dys):
-        groups = []
-        for dy in dys:
-            for dx in range(4):
-                if dy or dx:
-                    gather[4 * dy + dx].wait_recv()
-            group = lax.rem(y + 4 - dy, 4)
-            across[dy] = remote(err.at[core, group], err.at[core, group], sem_h, dy, sibling)
-            across[dy].start()
-            groups.append(group)
-        rows = jnp.concatenate([err[core, g] for g in groups], axis=0)
+    def code_grad(chunk):
+        for slot in range(16 * chunk + 1, 16 * chunk + 16):
+            gather[slot].wait_recv()
+        rows = slice(256 * chunk, 256 * chunk + 256)
+        across[chunk] = remote(err.at[core, rows], err.at[core, rows], sem_h, chunk, sibling)
+        across[chunk].start()
+        errors = err[core, rows, :]
+        groups = (2 * chunk, 2 * chunk + 1)
         for g in groups:
             grad_part[g] = jnp.zeros((64, 128), F32)
 
-        @pl.loop(0, 8)
+        @pl.loop(0, 8, unroll=True)
         def _(n):
             lats = pl.ds(pl.multiple_of(512 * n, 512), 512)
-            scores = lax.dot_general(dec2[lats, :], rows, NT, preferred_element_type=F32)
+            scores = lax.dot_general(dec2[lats, :], errors, NT, preferred_element_type=F32)
             for i, g in enumerate(groups):
                 where = key_t[:, pl.ds(pl.multiple_of(512 * core + 128 * g, 128), 128)]
                 total = grad_part[g]
@@ -244,8 +237,22 @@
                         where == 8 * n + b, scores[64 * b:64 * b + 64, 128 * i:128 * i + 128], 0.0)
                 grad_part[g] = total
 
-    code_grad((0, 1))
-    code_grad((2, 3))
+    recon(0)
+    recon(1)
+    for o in ORDER:
+        forwards[o].wait_recv()
+
+    @pl.loop(0, 8)
+    def _(j):
+        block = pl.ds(pl.multiple_of(128 * j, 128), 128)
+        cols_t[block, :] = cols[:, block].T
+
+    store_cols = pltpu.make_async_copy(cols_t, cols_out, sem_local.at[6])
+    store_cols.start()
+    error(0)
+    error(1)
+    code_grad(0)
+    code_grad(1)
 
     grads = {}
     for o in ORDER:
@@ -254,8 +261,8 @@
         grads[o].start()
 
     swap_codes.wait_recv()
-    for dy in range(4):
-        across[dy].wait_recv()
+    for chunk in range(2):
+        across[chunk].wait_recv()
 
     def tile(n):
         return pl.ds(pl.multiple_of(256 * n, 256), 256)
@@ -265,7 +272,7 @@
             [codes[h, g].astype(F32) for h in range(2) for g in range(4)], axis=1)
         errors = err[...].reshape(1024, 1024)
 
-        @pl.loop(first, last)
+        @pl.loop(first, last, unroll=True)
         def _(n):
             where = key_t[...]
             wide = jnp.concatenate(
@@ -273,10 +280,6 @@
             dec_grad_v[tile(n), :] = jnp.dot(wide, errors, preferred_element_type=F32).astype(BF16)
             pltpu.make_async_copy(dec_grad_v.at[tile(n)], dec_grad_out.at[tile(n)], sem_o.at[n]).start()
 
-    for o in ORDER:
-        forwards[o].wait_recv()
-    store_cols = pltpu.make_async_copy(cols, cols_out, sem_local.at[6])
-    store_cols.start()
     dec_grads(0, 4)
     total = grad_part[z]
     for o in ORDER:
@@ -297,9 +300,9 @@
     for copy in shares:
         copy.wait()
     for o in ORDER:
-        for group in (sends, forwards, returns, shared, grads):
+        for group in (forwards, returns, shared, grads):
             group[o].wait_send()
-    for copy in [give_bias, give_dec, swap_codes] + list(scatter.values()) + list(gather.values()) + list(across.values()):
+    for copy in [sends[2], give_bias, give_dec, swap_codes] + list(scatter.values()) + list(gather.values()) + list(across.values()):
         copy.wait_send()
     store_cols.wait()
 
@@ -308,34 +311,41 @@
         pltpu.make_async_copy(dec_grad_v.at[tile(n)], dec_grad_out.at[tile(n)], sem_o.at[n]).wait()
 
 
-def enc_grads(cols, grad, idx_t, lat_ref, dec_in, enc_out, enc_bias_out, dec_out, grad2, key):
+def enc_grads(cols_t, grad, idx_t, lat_ref, dec_in, enc_out, enc_bias_out, dec_out, wide, sem):
     n = pl.program_id(0)
 
     @pl.when(n == 0)
     def _():
+        pltpu.make_async_copy(dec_in, dec_out, sem).start()
         odd = (lax.broadcasted_iota(I32, (128, 128), 1) >= 64).astype(I32)
+        sums = [jnp.zeros((1, 128), F32)] * 16
         for g in range(8):
             piece = lax.shift_right_logical(idx_t[:, 128 * g:128 * g + 128], 6) - 32 * lat_ref[0]
-            key[128 * g:128 * g + 128, :] = jnp.concatenate([piece, piece], axis=0).T - odd
+            where = jnp.concatenate([piece, piece], axis=0).T - odd
             piece = grad[g % 2, g // 2]
-            grad2[128 * g:128 * g + 128, :] = jnp.concatenate([piece, piece], axis=0).T
-
-    where, values = key[...], grad2[...]
-    wide = [jnp.where(where == 8 * n + 2 * j, values, 0.0) for j in range(4)]
-    for j in range(4):
-        enc_bias_out[:, 128 * j:128 * j + 128] = jnp.sum(wide[j], axis=0, keepdims=True)
-    wide = jnp.concatenate([w.astype(BF16) for w in wide], axis=1)
-    enc_out[...] = lax.dot_general(
-        cols[...], wide, (((0,), (0,)), ((), ())), preferred_element_type=F32).astype(BF16)
-    dec_out[...] = dec_in[...]
+            values = jnp.concatenate([piece, piece], axis=0).T
+            for j in range(16):
+                part = jnp.where(where == 2 * j, values, 0.0)
+                sums[j] = sums[j] + jnp.sum(part, axis=0, keepdims=True)
+                wide[128 * g:128 * g + 128, 128 * j:128 * j + 128] = part.astype(BF16)
+        for j in range(16):
+            enc_bias_out[:, 128 * j:128 * j + 128] = sums[j]
+
+    tile = pl.ds(pl.multiple_of(512 * n, 512), 512)
+    enc_out[...] = jnp.dot(cols_t[...], wide[:, tile], preferred_element_type=F32).astype(BF16)
+
+    @pl.when(n == 3)
+    def _():
+        pltpu.make_async_copy(dec_in, dec_out, sem).wait()
 
 
 def local(tokens, indices, enc_weight, dec_weight, enc_bias, dec_bias):
     idx_t = indices.T
     vmem = pl.BlockSpec(memory_space=pltpu.VMEM)
-    hbm = pl.BlockSpec(memory_space=pl.ANY)
+    hbm = pl.BlockSpec(memory_space=pltpu.HBM)
+    free = pl.BlockSpec(memory_space=pl.ANY)
     dma = pltpu.SemaphoreType.DMA
-    cols, dec_grad, grad, bias_grad = pl.pallas_call(
+    cols_t, dec_grad, grad, bias_grad = pl.pallas_call(
         exchange,
         out_shape=[
             jax.ShapeDtypeStruct((1024, 1024), BF16),
@@ -344,7 +354,7 @@
             jax.ShapeDtypeStruct((1, 1024), F32),
         ],
         in_specs=[hbm] * 6,
-        out_specs=[hbm, hbm, vmem, vmem],
+        out_specs=[free, free, vmem, vmem],
         scratch_shapes=[
             pltpu.VMEM((64, 1024), I32),
             pltpu.VMEM((2, 1, 2048), F32),
@@ -360,20 +370,21 @@
             pltpu.VMEM((4, 64, 128), F32),
             pltpu.VMEM((2, 4, 64, 128), BF16),
             pltpu.VMEM((256, 4096), BF16),
-            pltpu.VMEM((128, 1024), F32),
-            pltpu.VMEM((2, 256, 1024), BF16),
-            pltpu.VMEM((16, 32, 1024), BF16),
-            pltpu.VMEM((2, 4, 128, 1024), BF16),
+            pltpu.VMEM((1024, 1024), BF16),
+            pltpu.VMEM((512, 1024), BF16),
+            pltpu.VMEM((32, 16, 1024), BF16),
+            pltpu.VMEM((2, 512, 1024), BF16),
             pltpu.VMEM((4, 64, 128), F32),
             pltpu.VMEM((4, 64, 128), F32),
             pltpu.VMEM((2048, 1024), BF16),
             dma((7,)), dma((2, 4)), dma((2, 3)), dma((2, 4)), dma((2, 4)), dma((2, 4)), dma((2, 1)),
-            dma((2, 16)), dma((2, 16)), dma((2, 4)), dma((2, 4)), dma((2, 8)), dma((8,)),
+            dma((2, 32)), dma((2, 32)), dma((2, 2)), dma((2, 4)), dma((2, 8)), dma((8,)),
         ],
         compiler_params=pltpu.CompilerParams(
-            collective_id=0, has_side_effects=True, vmem_limit_bytes=58 * 2**20),
+            collective_id=0, has_side_effects=True, vmem_limit_bytes=42 * 2**20),
         name="exchange",
-    )(tokens, idx_t, enc_weight, dec_weight, enc_bias[None, :], dec_bias[None, :])
+    )(*[pltpu.with_memory_space_constraint(a, pltpu.HBM) for a in (
+        tokens, idx_t, enc_weight, dec_weight, enc_bias[None, :], dec_bias[None, :])])
 
     enc_grad, enc_bias_grad, dec_grad = pl.pallas_call(
         enc_grads,
@@ -384,21 +395,21 @@
             jax.ShapeDtypeStruct((2048, 1024), BF16),
         ],
         in_specs=[
-            pl.BlockSpec((1024, 1024), lambda n: (0, 0)),
-            pl.BlockSpec((2, 4, 64, 128), lambda n: (0, 0, 0, 0)),
-            pl.BlockSpec((64, 1024), lambda n: (0, 0)),
+            vmem,
+            vmem,
+            vmem,
             pl.BlockSpec(memory_space=pltpu.SMEM),
-            pl.BlockSpec((512, 1024), lambda n: (n, 0)),
+            free,
         ],
         out_specs=[
             pl.BlockSpec((1024, 512), lambda n: (0, n)),
-            pl.BlockSpec((1, 512), lambda n: (0, n)),
-            pl.BlockSpec((512, 1024), lambda n: (n, 0)),
+            pl.BlockSpec((1, 2048), lambda n: (0, 0)),
+            hbm,
         ],
-        scratch_shapes=[pltpu.VMEM((1024, 128), F32), pltpu.VMEM((1024, 128), I32)],
-        compiler_params=pltpu.CompilerParams(vmem_limit_bytes=58 * 2**20),
+        scratch_shapes=[pltpu.VMEM((1024, 2048), BF16), dma(())],
+        compiler_params=pltpu.CompilerParams(vmem_limit_bytes=40 * 2**20),
         name="enc_grads",
-    )(cols, grad, idx_t, lax.axis_index("lat").reshape(1), dec_grad)
+    )(cols_t, grad, idx_t, lax.axis_index("lat").reshape(1), dec_grad)
     return enc_grad, dec_grad, enc_bias_grad[0], bias_grad[0]
 
 

time: 89.9 us -> 80.8 us (0.90)
  Pallas kernels: 87.4 us -> 78.4 us
    pallas_call x1, Pallas kernels: 77.7 us -> 70.9 us  [local(): pl.pallas_call(exchange, out_shape=[jax.ShapeDtypeStruct((1024, 1024), BF...]
    pallas_call x1, Pallas kernels: 9.68 us -> 7.51 us  [local(): pl.pallas_call(enc_grads, grid=(4,), out_shape=[jax.ShapeDtypeStruct((102...]
where the time goes in v4:
time: 80.8 us; the launch traced here: 79.6 us
  Pallas kernels  78.4 us (97%)
    pallas_call x1, Pallas kernels, local(): pl.pallas_call(exchange, out_shape=[jax.ShapeDtypeStruct((1024, 1024), BF...  70.9 us
    pallas_call x1, Pallas kernels, local(): pl.pallas_call(enc_grads, grid=(4,), out_shape=[jax.ShapeDtypeStruct((102...  7.51 us

profile of v4, /device:TPU:0, one launch (start us, length us, event | category | flops | bytes accessed | tf_op | source)
XLA Modules:
  0.0 79.6 jit_solution(11382642846819104505)
XLA Ops:
  0.6 0.0 copy-start
  0.6 70.9 %exchange.1 = (bf16[1024,1024]{1,0:T(8,128)(2,1)S(1)}, bf16[2048,1024]{1,0:T(8,128)(2,1)S(1)}, f32[2,4,64,128]{3,2,1,0:T(8,128)S(1)}, f32[1,1024]{1,0:T(1,128)S(1)}) custom-call(bf16[256,4096]{1,0:T(8,128)(2,1)} %tokens.1, s32[64,1024]{1,0:T(8,128)} %bitcast.6, bf16[1024,2048]{1,0:T(8,128)(2,1)} %enc.1, bf16[2048,1024]{1,0:T(8,128)(2,1)} %dec.1, ...), custom_call_target="tpu_custom_call" | custom-call | tf_op jit(solution)/shard_map/exchange/pallas_call | solution.py:348
  71.5 0.0 copy-done
  71.5 7.5 %enc_grads.1 = (bf16[1024,2048]{1,0:T(8,128)(2,1)}, f32[1,2048]{1,0:T(1,128)}, bf16[2048,1024]{1,0:T(8,128)(2,1)}) custom-call(bf16[1024,1024]{1,0:T(8,128)(2,1)S(1)} %get-tuple-element.11.cols_t, f32[2,4,64,128]{3,2,1,0:T(8,128)S(1)} %get-tuple-element.12.grad, s32[64,1024]{1,0:T(8,128)S(1)} %bitcast.7, s32[1]{0:T(128)} %bitcast.3.lat_ref, ...), custom_call_target="tpu_custom_call" | custom-call | tf_op jit(solution)/shard_map/enc_grads/pallas_call | solution.py:389
  79.0 0.6 copy.11
Async XLA Ops:
  0.6 70.9 %copy-start = (s32[1024,64]{0,1:T(8,128)S(1)}, s32[1024,64]{0,1:T(8,128)}, u32[]{:S(2)}) copy-start(s32[1024,64]{0,1:T(8,128)} %param.7) | copy-start | bytes 786436

commit v5 on v4

--- a/solution.py
+++ b/solution.py
@@ -191,15 +191,19 @@
                 dense[128 * pos:128 * pos + 128, 128 * j:128 * j + 128] = jnp.where(
                     where == 2 * j, values, 0.0).astype(BF16)
 
-        @pl.loop(0, 2, unroll=True)
-        def _(n):
-            base = pl.ds(pl.multiple_of(512 * n, 512), 512)
-            rs_send[256 * chunk:256 * chunk + 256, base] = jnp.dot(
+        rows = slice(256 * chunk, 256 * chunk + 256)
+        for n in range(2):
+            base = slice(512 * n, 512 * n + 512)
+            rs_send[rows, base] = jnp.dot(
                 dense[...], dec2[:, base], preferred_element_type=F32).astype(BF16)
-
-        for slot, place, device in partners(chunk):
-            scatter[slot] = remote(rs_send.at[share(chunk, place)], rs_recv.at[slot], sem_r, slot, device)
-            scatter[slot].start()
+            if chunk == 1 and n == 0:
+                continue
+            base = base if chunk == 0 else slice(0, 1024)
+            for slot, place, device in partners(chunk):
+                scatter[slot, n] = remote(
+                    rs_send.at[share(chunk, place), base], rs_recv.at[slot, :, base], sem_r,
+                    slot + 32 * (n if chunk == 0 else 0), device)
+                scatter[slot, n].start()
 
     def error(chunk):
         mine = share(chunk, spot)
@@ -207,7 +211,8 @@
         full = rs_send[mine, :].astype(F32) + bias_d[...]
         full = full - cols[rows, :].astype(F32)
         for slot in range(16 * chunk + 1, 16 * chunk + 16):
-            scatter[slot].wait_recv()
+            for n in range(chunk, 2):
+                scatter[slot, n].wait_recv()
             full = full + rs_recv[slot].astype(F32)
         err[core, mine, :] = full.astype(BF16)
         for slot, _, device in partners(chunk):
@@ -311,32 +316,31 @@
         pltpu.make_async_copy(dec_grad_v.at[tile(n)], dec_grad_out.at[tile(n)], sem_o.at[n]).wait()
 
 
-def enc_grads(cols_t, grad, idx_t, lat_ref, dec_in, enc_out, enc_bias_out, dec_out, wide, sem):
-    n = pl.program_id(0)
-
-    @pl.when(n == 0)
-    def _():
-        pltpu.make_async_copy(dec_in, dec_out, sem).start()
-        odd = (lax.broadcasted_iota(I32, (128, 128), 1) >= 64).astype(I32)
-        sums = [jnp.zeros((1, 128), F32)] * 16
-        for g in range(8):
-            piece = lax.shift_right_logical(idx_t[:, 128 * g:128 * g + 128], 6) - 32 * lat_ref[0]
-            where = jnp.concatenate([piece, piece], axis=0).T - odd
-            piece = grad[g % 2, g // 2]
-            values = jnp.concatenate([piece, piece], axis=0).T
-            for j in range(16):
-                part = jnp.where(where == 2 * j, values, 0.0)
-                sums[j] = sums[j] + jnp.sum(part, axis=0, keepdims=True)
-                wide[128 * g:128 * g + 128, 128 * j:128 * j + 128] = part.astype(BF16)
-        for j in range(16):
-            enc_bias_out[:, 128 * j:128 * j + 128] = sums[j]
-
-    tile = pl.ds(pl.multiple_of(512 * n, 512), 512)
-    enc_out[...] = jnp.dot(cols_t[...], wide[:, tile], preferred_element_type=F32).astype(BF16)
-
-    @pl.when(n == 3)
-    def _():
-        pltpu.make_async_copy(dec_in, dec_out, sem).wait()
+def enc_grads(
+    cols_t, grad, idx_t, bias_in, lat_ref, dec_in, enc_out, enc_bias_out, bias_out, dec_out, key, values, wide, enc_v, sem
+):
+    pass_dec = pltpu.make_async_copy(dec_in, dec_out, sem.at[4])
+    pass_dec.start()
+    bias_out[...] = bias_in[...]
+    odd = (lax.broadcasted_iota(I32, (128, 128), 1) >= 64).astype(I32)
+    for g in range(8):
+        piece = lax.shift_right_logical(idx_t[:, 128 * g:128 * g + 128], 6) - 32 * lat_ref[0]
+        key[128 * g:128 * g + 128, :] = jnp.concatenate([piece, piece], axis=0).T - odd
+        piece = grad[g % 2, g // 2]
+        values[128 * g:128 * g + 128, :] = jnp.concatenate([piece, piece], axis=0).T
+
+    stores = []
+    for n in range(4):
+        for j in range(4 * n, 4 * n + 4):
+            part = jnp.where(key[...] == 2 * j, values[...], 0.0)
+            enc_bias_out[:, 128 * j:128 * j + 128] = jnp.sum(part, axis=0, keepdims=True)
+            wide[:, 128 * j:128 * j + 128] = part.astype(BF16)
+        tile = slice(512 * n, 512 * n + 512)
+        enc_v[n] = jnp.dot(cols_t[...], wide[:, tile], preferred_element_type=F32).astype(BF16)
+        stores.append(pltpu.make_async_copy(enc_v.at[n], enc_out.at[:, tile], sem.at[n]))
+        stores[n].start()
+    for copy in stores + [pass_dec]:
+        copy.wait()
 
 
 def local(tokens, indices, enc_weight, dec_weight, enc_bias, dec_bias):
@@ -378,7 +382,7 @@
             pltpu.VMEM((4, 64, 128), F32),
             pltpu.VMEM((2048, 1024), BF16),
             dma((7,)), dma((2, 4)), dma((2, 3)), dma((2, 4)), dma((2, 4)), dma((2, 4)), dma((2, 1)),
-            dma((2, 32)), dma((2, 32)), dma((2, 2)), dma((2, 4)), dma((2, 8)), dma((8,)),
+            dma((2, 48)), dma((2, 32)), dma((2, 2)), dma((2, 4)), dma((2, 8)), dma((8,)),
         ],
         compiler_params=pltpu.CompilerParams(
             collective_id=0, has_side_effects=True, vmem_limit_bytes=42 * 2**20),
@@ -386,30 +390,26 @@
     )(*[pltpu.with_memory_space_constraint(a, pltpu.HBM) for a in (
         tokens, idx_t, enc_weight, dec_weight, enc_bias[None, :], dec_bias[None, :])])
 
-    enc_grad, enc_bias_grad, dec_grad = pl.pallas_call(
+    enc_grad, enc_bias_grad, bias_grad, dec_grad = pl.pallas_call(
         enc_grads,
-        grid=(4,),
         out_shape=[
             jax.ShapeDtypeStruct((1024, 2048), BF16),
             jax.ShapeDtypeStruct((1, 2048), F32),
+            jax.ShapeDtypeStruct((1, 1024), F32),
             jax.ShapeDtypeStruct((2048, 1024), BF16),
         ],
-        in_specs=[
-            vmem,
-            vmem,
-            vmem,
-            pl.BlockSpec(memory_space=pltpu.SMEM),
-            free,
+        in_specs=[vmem, vmem, vmem, vmem, pl.BlockSpec(memory_space=pltpu.SMEM), free],
+        out_specs=[hbm, vmem, vmem, hbm],
+        scratch_shapes=[
+            pltpu.VMEM((1024, 128), I32),
+            pltpu.VMEM((1024, 128), F32),
+            pltpu.VMEM((1024, 2048), BF16),
+            pltpu.VMEM((4, 1024, 512), BF16),
+            dma((5,)),
         ],
-        out_specs=[
-            pl.BlockSpec((1024, 512), lambda n: (0, n)),
-            pl.BlockSpec((1, 2048), lambda n: (0, 0)),
-            hbm,
-        ],
-        scratch_shapes=[pltpu.VMEM((1024, 2048), BF16), dma(())],
         compiler_params=pltpu.CompilerParams(vmem_limit_bytes=40 * 2**20),
         name="enc_grads",
-    )(cols_t, grad, idx_t, lax.axis_index("lat").reshape(1), dec_grad)
+    )(cols_t, grad, idx_t, bias_grad, lax.axis_index("lat").reshape(1), dec_grad)
     return enc_grad, dec_grad, enc_bias_grad[0], bias_grad[0]
 
 

time: 80.8 us -> 79.2 us (0.980)
  Pallas kernels: 78.4 us -> 77.2 us
    pallas_call x1, Pallas kernels: 7.51 us -> 6.54 us  [local(): pl.pallas_call(enc_grads, out_shape=[jax.ShapeDtypeStruct((1024, 2048), B...]
where the time goes in v5:
time: 79.2 us; the launch traced here: 78 us
  Pallas kernels  77.2 us (97%)
  between operations  0.84 us (1%)
    pallas_call x1, Pallas kernels, local(): pl.pallas_call(exchange, out_shape=[jax.ShapeDtypeStruct((1024, 1024), BF...  70.6 us
    pallas_call x1, Pallas kernels, local(): pl.pallas_call(enc_grads, out_shape=[jax.ShapeDtypeStruct((1024, 2048), B...  6.54 us

profile of v5, /device:TPU:0, one launch (start us, length us, event | category | flops | bytes accessed | tf_op | source)
XLA Modules:
  0.0 78.0 jit_solution(2029527878124899168)
XLA Ops:
  0.6 0.0 copy-start
  0.6 70.6 %exchange.1 = (bf16[1024,1024]{1,0:T(8,128)(2,1)S(1)}, bf16[2048,1024]{1,0:T(8,128)(2,1)S(1)}, f32[2,4,64,128]{3,2,1,0:T(8,128)S(1)}, f32[1,1024]{1,0:T(1,128)S(1)}) custom-call(bf16[256,4096]{1,0:T(8,128)(2,1)} %tokens.1, s32[64,1024]{1,0:T(8,128)} %bitcast.6, bf16[1024,2048]{1,0:T(8,128)(2,1)} %enc.1, bf16[2048,1024]{1,0:T(8,128)(2,1)} %dec.1, ...), custom_call_target="tpu_custom_call" | custom-call | tf_op jit(solution)/shard_map/exchange/pallas_call | solution.py:352
  71.3 0.0 copy-done
  71.3 6.5 %enc_grads.1 = (bf16[1024,2048]{1,0:T(8,128)(2,1)}, f32[1,2048]{1,0:T(1,128)}, f32[1,1024]{1,0:T(1,128)}, bf16[2048,1024]{1,0:T(8,128)(2,1)}) custom-call(bf16[1024,1024]{1,0:T(8,128)(2,1)S(1)} %get-tuple-element.12.cols_t, f32[2,4,64,128]{3,2,1,0:T(8,128)S(1)} %get-tuple-element.13.grad, s32[64,1024]{1,0:T(8,128)S(1)} %bitcast.7, ...), custom_call_target="tpu_custom_call" | custom-call | tf_op jit(solution)/shard_map/enc_grads/pallas_call | solution.py:393
Async XLA Ops:
  0.6 70.7 %copy-start = (s32[1024,64]{0,1:T(8,128)S(1)}, s32[1024,64]{0,1:T(8,128)}, u32[]{:S(2)}) copy-start(s32[1024,64]{0,1:T(8,128)} %param.7) | copy-start | bytes 786436

commit v6 on v5

--- a/solution.py
+++ b/solution.py
@@ -170,8 +170,15 @@
     swap_codes = remote(codes.at[core], codes.at[core], sem_k, 0, sibling)
     swap_codes.start()
 
-    spot = 4 * y + x
+    near, far = jnp.where(core == 0, x, y), jnp.where(core == 0, y, x)
+    spot = 4 * near + far
     scatter, gather, across = {}, {}, {}
+
+    def first(o):
+        return in_plane(o * core, o * other)
+
+    def second(o):
+        return in_plane(o * other, o * core)
 
     def share(chunk, place):
         return pl.ds(pl.multiple_of(256 * chunk + 16 * place, 16), 16)
@@ -179,7 +186,8 @@
     def partners(chunk):
         for slot in range(1, 16):
             dy, dx = PLANE[slot]
-            place = 4 * lax.rem(y + dy, 4) + lax.rem(x + dx, 4)
+            row, column = lax.rem(y + dy, 4), lax.rem(x + dx, 4)
+            place = jnp.where(core == 0, 4 * column + row, 4 * row + column)
             yield 16 * chunk + slot, place, in_plane(dy, dx)
 
     def recon(chunk):
@@ -215,13 +223,27 @@
                 scatter[slot, n].wait_recv()
             full = full + rs_recv[slot].astype(F32)
         err[core, mine, :] = full.astype(BF16)
-        for slot, _, device in partners(chunk):
-            gather[slot] = remote(err.at[core, mine], err.at[core, mine], sem_g, slot, device)
-            gather[slot].start()
+        for o in ORDER:
+            gather[chunk, 0, o] = remote(
+                err.at[core, mine], err.at[core, mine], sem_g, 16 * chunk + o, second(o))
+            gather[chunk, 0, o].start()
+        hand_on(chunk, mine, 0)
+
+    def hand_on(chunk, rows, source):
+        for o in ORDER:
+            gather[chunk, o, source] = remote(
+                err.at[core, rows], err.at[core, rows], sem_g, 16 * chunk + 4 * o + source, first(o))
+            gather[chunk, o, source].start()
+
+    def pass_on(chunk):
+        for source in ORDER:
+            gather[chunk, 0, source].wait_recv()
+            hand_on(chunk, share(chunk, 4 * near + lax.rem(far + 4 - source, 4)), source)
 
     def code_grad(chunk):
-        for slot in range(16 * chunk + 1, 16 * chunk + 16):
-            gather[slot].wait_recv()
+        for source in (0,) + ORDER:
+            for o in ORDER:
+                gather[chunk, o, source].wait_recv()
         rows = slice(256 * chunk, 256 * chunk + 256)
         across[chunk] = remote(err.at[core, rows], err.at[core, rows], sem_h, chunk, sibling)
         across[chunk].start()
@@ -256,6 +278,8 @@
     store_cols.start()
     error(0)
     error(1)
+    pass_on(0)
+    pass_on(1)
     code_grad(0)
     code_grad(1)
 

time: 79.2 us -> 79.6 us (level)
  no operation moved by 1% of the time
where the time goes in v6:
time: 79.6 us; the launch traced here: 78.4 us
  Pallas kernels  77.6 us (97%)
  between operations  0.84 us (1%)
    pallas_call x1, Pallas kernels, local(): pl.pallas_call(exchange, out_shape=[jax.ShapeDtypeStruct((1024, 1024), BF...  71 us
    pallas_call x1, Pallas kernels, local(): pl.pallas_call(enc_grads, out_shape=[jax.ShapeDtypeStruct((1024, 2048), B...  6.54 us

profile of v6, /device:TPU:0, one launch (start us, length us, event | category | flops | bytes accessed | tf_op | source)
XLA Modules:
  0.0 78.4 jit_solution(11798946400285897416)
XLA Ops:
  0.6 0.0 copy-start
  0.6 71.0 %exchange.1 = (bf16[1024,1024]{1,0:T(8,128)(2,1)S(1)}, bf16[2048,1024]{1,0:T(8,128)(2,1)S(1)}, f32[2,4,64,128]{3,2,1,0:T(8,128)S(1)}, f32[1,1024]{1,0:T(1,128)S(1)}) custom-call(bf16[256,4096]{1,0:T(8,128)(2,1)} %tokens.1, s32[64,1024]{1,0:T(8,128)} %bitcast.6, bf16[1024,2048]{1,0:T(8,128)(2,1)} %enc.1, bf16[2048,1024]{1,0:T(8,128)(2,1)} %dec.1, ...), custom_call_target="tpu_custom_call" | custom-call | tf_op jit(solution)/shard_map/exchange/pallas_call | solution.py:376
  71.7 0.0 copy-done
  71.7 6.5 %enc_grads.1 = (bf16[1024,2048]{1,0:T(8,128)(2,1)}, f32[1,2048]{1,0:T(1,128)}, f32[1,1024]{1,0:T(1,128)}, bf16[2048,1024]{1,0:T(8,128)(2,1)}) custom-call(bf16[1024,1024]{1,0:T(8,128)(2,1)S(1)} %get-tuple-element.12.cols_t, f32[2,4,64,128]{3,2,1,0:T(8,128)S(1)} %get-tuple-element.13.grad, s32[64,1024]{1,0:T(8,128)S(1)} %bitcast.7, ...), custom_call_target="tpu_custom_call" | custom-call | tf_op jit(solution)/shard_map/enc_grads/pallas_call | solution.py:417
Async XLA Ops:
  0.6 71.1 %copy-start = (s32[1024,64]{0,1:T(8,128)S(1)}, s32[1024,64]{0,1:T(8,128)}, u32[]{:S(2)}) copy-start(s32[1024,64]{0,1:T(8,128)} %param.7) | copy-start | bytes 786436
